TPU v7x, 512 devices: a whole 4x8x8 slice. The times are simulated.
512 devices in a mesh: kvp: 64 (over y, x, core), tp: 8 (over z).
Axes of the slice: x: 4, y: 8, z: 8, core: 2. Of those that a mesh axis runs over, the one named last changes fastest.
Arguments:
- queries: bfloat16 [2, 16, 128, 128], P(None, None, 'tp', 'kvp'), may hold values from -8 to 8
- fresh_kv: bfloat16 [2, 16, 2, 8, 128], P(None, None, None, 'tp', 'kvp'), may hold values from -8 to 8
- kv_cache: bfloat16 [4096, 2, 8, 1024], P('kvp', None, None, 'tp'), may hold values from -8 to 8
- page_owner: int32 [4096], replicated, may hold values from 0 to 63, as said below
- context_pages: int32 [16], replicated, may hold values from 1 to 512, 4096 in all
- residual: bfloat16 [32, 16384], P(None, ('kvp', 'tp')), may hold values from -8 to 8
- out_proj: bfloat16 [16384, 16384], P('tp', 'kvp'), may hold values from -0.046875 to 0.046875
- norm_gain: bfloat16 [16384], P(('kvp', 'tp')), may hold values from 0.099609375 to 1.8984375
- gate_weight: bfloat16 [64, 256, 26624], P(None, 'tp', 'kvp'), may hold values from -0.046875 to 0.046875
- up_weight: bfloat16 [64, 256, 26624], P(None, 'tp', 'kvp'), may hold values from -0.046875 to 0.046875
Outputs:
- regrouped: bfloat16 [4096, 2, 8, 1024], P('kvp', None, None, 'tp')
- stream: bfloat16 [32, 16384], P(None, ('kvp', 'tp'))
- hidden: bfloat16 [32, 26624], P(None, ('kvp', 'tp'))
Inputs may be any that keep to these rules, and one draw needn't show every extreme that they name: `page_owner`: each device's contiguous block of 64 pages names every owner exactly 1 times.
All inputs are finite; a program needn't handle non-finite values.
Results may differ from a plain program's by a relative error of at most 0.035.
Values may be sent and summed in bfloat16 or wider, within the bound.
No kernel may reach another device: no remote copies, remote signals or barrier semaphores. Data moves between devices by JAX's collectives and lax.ppermute only.
A program may use at most 64 MiB of HBM per device.

v0:
```python
import jax
import jax.numpy as jnp
from jax import lax
from jax.sharding import PartitionSpec as P

D = 16384
HEADS = 128
KVH = 8
HD = 128


negative = -1e30
epsilon = 1e-05


def merged(array, axis, combine):
    everything = jax.tree.map(lambda part: lax.all_gather(part, axis), array)
    leading = jax.tree.map(lambda part: part[0], everything)

    def turn(k, so_far):
        return combine(so_far, jax.tree.map(lambda part: part[k], everything))

    return lax.fori_loop(1, lax.axis_size(axis), turn, leading)


def merge_pair(earlier, later):
    peak_a, sum_a, num_a = earlier
    peak_b, sum_b, num_b = later
    peak = jnp.maximum(peak_a, peak_b)
    factor_a = jnp.exp(peak_a - peak)
    factor_b = jnp.exp(peak_b - peak)
    return (
        peak,
        sum_a * factor_a + sum_b * factor_b,
        num_a * factor_a[..., None] + num_b * factor_b[..., None],
    )


def finish_flat(peak, denom, numerator, fresh_scores, fresh_values):
    new_peak = jnp.maximum(peak, jnp.max(fresh_scores, axis=1))
    carried = jnp.exp(peak - new_peak)
    fresh_weights = jnp.exp(fresh_scores - new_peak[:, None])
    denom = denom * carried + jnp.sum(fresh_weights, axis=1)
    numerator = numerator * carried[:, None] + jnp.einsum(
        "iu,iud->id",
        fresh_weights.astype(jnp.bfloat16),
        fresh_values,
        preferred_element_type=jnp.float32,
    )
    return (numerator / denom[:, None]).astype(jnp.bfloat16)


def shards(
    queries,
    fresh_kv,
    kv_cache,
    page_owner,
    context_pages,
    residual,
    out_proj,
    norm_gain,
    gate_weight,
    up_weight,
):
    kvp_index = lax.axis_index("kvp")
    pages_dev = kv_cache.shape[0]
    page_len = kv_cache.shape[2]
    kv_local = kv_cache.shape[3] // HD
    group_size = HEADS // KVH
    num_steps = queries.shape[0]
    num_rows = queries.shape[1]
    score_scale = HD ** (-0.5)
    highest = lax.Precision.HIGHEST
    all_queries, all_fresh = (
        lax.all_gather(queries, "kvp", axis=3, tiled=True),
        lax.all_gather(fresh_kv, "kvp", axis=4, tiled=True),
    )
    own_block = lax.dynamic_slice_in_dim(page_owner, kvp_index * pages_dev, pages_dev)
    outgoing = jnp.take(kv_cache, jnp.argsort(own_block, stable=True), axis=0)
    regrouped = lax.all_to_all(outgoing, "kvp", split_axis=0, concat_axis=0, tiled=True)
    ordered = jnp.argsort(page_owner, stable=True)
    page_ids = lax.dynamic_slice_in_dim(ordered, kvp_index * pages_dev, pages_dev)
    starts = jnp.cumsum(context_pages) - context_pages
    member = (starts[None, :] <= page_ids[:, None]) & (
        page_ids[:, None] < (starts + context_pages)[None, :]
    )
    row_of = jnp.sum(jnp.where(member, jnp.arange(num_rows, dtype=jnp.int32)[None, :], 0), axis=1)
    query_all = all_queries.reshape(num_steps, num_rows, kv_local, group_size, HD)
    cache = regrouped.reshape(pages_dev, 2, page_len, kv_local, HD)
    page_keys = cache[:, 0]
    page_values = cache[:, 1]
    query_pages = jnp.take(query_all, row_of, axis=1)
    scores = (
        jnp.einsum("spkgd,ptkd->pkgst", query_pages, page_keys, preferred_element_type=jnp.float32)
        * score_scale
    )
    page_peak = jnp.max(scores, axis=4)
    row_peak = jnp.max(
        jnp.where(member[:, :, None, None, None], page_peak[:, None], negative), axis=0
    )
    page_weights = jnp.exp(scores - jnp.take(row_peak, row_of, axis=0)[..., None])
    page_sum = jnp.sum(page_weights, axis=4)
    page_num = jnp.einsum(
        "pkgst,ptkd->pkgsd",
        page_weights.astype(jnp.bfloat16),
        page_values,
        preferred_element_type=jnp.float32,
    )
    onehot = member.astype(jnp.float32)
    row_sum = jnp.dot(onehot.T, page_sum.reshape(pages_dev, -1), precision=highest)
    row_num = jnp.dot(onehot.T, page_num.reshape(pages_dev, -1), precision=highest).reshape(
        num_rows, -1, HD
    )
    row_peak = row_peak.reshape(num_rows, -1)
    fresh_keys = all_fresh[:, :, 0]
    fresh_values = all_fresh[:, :, 1]
    fresh_scores = (
        jnp.einsum("srkgd,urkd->rkgsu", query_all, fresh_keys, preferred_element_type=jnp.float32)
        * score_scale
    )
    causal = (
        jnp.arange(num_steps, dtype=jnp.int32)[:, None]
        >= jnp.arange(num_steps, dtype=jnp.int32)[None, :]
    )
    fresh_scores = jnp.where(causal, fresh_scores, negative)
    total = num_rows * kv_local * group_size * num_steps
    flat_fresh_scores = fresh_scores.reshape(total, num_steps)
    flat_fresh_values = jnp.broadcast_to(
        fresh_values.transpose(1, 2, 0, 3)[:, :, None, None],
        (num_rows, kv_local, group_size, num_steps, num_steps, HD),
    ).reshape(total, num_steps, HD)
    peak, denom, numerator = merged((row_peak, row_sum, row_num), "kvp", merge_pair)
    flat_attended = finish_flat(
        peak.reshape(-1),
        denom.reshape(-1),
        numerator.reshape(total, HD),
        flat_fresh_scores,
        flat_fresh_values,
    )
    attended = flat_attended.reshape(num_rows, kv_local, group_size, num_steps, HD)
    attended = attended.transpose(3, 0, 1, 2, 4).reshape(
        num_steps * num_rows, kv_local * group_size * HD
    )
    partial_value = jnp.dot(attended, out_proj, preferred_element_type=jnp.float32)
    projected = lax.psum_scatter(
        partial_value.astype(jnp.bfloat16), "tp", scatter_dimension=1, tiled=True
    ).astype(jnp.float32)
    stream = (residual.astype(jnp.float32) + projected).astype(jnp.bfloat16)
    flat_gate = gate_weight.reshape(-1, gate_weight.shape[2])
    flat_up = up_weight.reshape(-1, up_weight.shape[2])
    batch_rows = stream.shape[0]
    columns = lax.all_gather(stream, "kvp", axis=1, tiled=True)
    gain_piece = lax.all_gather(norm_gain.reshape(1, -1), "kvp", axis=1, tiled=True)
    widened = columns.astype(jnp.float32)
    squares = jnp.sum(widened * widened, axis=1)
    scaled = (widened * gain_piece.astype(jnp.float32)).astype(jnp.bfloat16)
    gate_acc = jnp.dot(scaled, flat_gate, preferred_element_type=jnp.float32)
    up_acc = jnp.dot(scaled, flat_up, preferred_element_type=jnp.float32)
    gate_acc, up_acc, squares = (gate_acc, up_acc, squares)
    tp_parts = lax.axis_size("tp")
    tiled = jnp.broadcast_to(squares[:, None], (batch_rows, tp_parts))
    gate_part, up_part, square_total = (
        lax.psum_scatter(
            gate_acc.astype(jnp.bfloat16), "tp", scatter_dimension=1, tiled=True
        ).astype(jnp.float32),
        lax.psum_scatter(up_acc.astype(jnp.bfloat16), "tp", scatter_dimension=1, tiled=True).astype(
            jnp.float32
        ),
        lax.psum_scatter(tiled.astype(jnp.bfloat16), "tp", scatter_dimension=1, tiled=True).astype(
            jnp.float32
        ),
    )
    inverse = lax.rsqrt(square_total[:, 0] / D + epsilon)
    gated = gate_part * inverse[:, None]
    lifted = up_part * inverse[:, None]
    hidden = (jax.nn.silu(gated) * lifted).astype(jnp.bfloat16)
    return (regrouped, stream, hidden)


def solution(mesh):
    return jax.shard_map(
        shards,
        mesh=mesh,
        in_specs=(
            P(None, None, "tp", "kvp"),
            P(None, None, None, "tp", "kvp"),
            P("kvp", None, None, "tp"),
            P(),
            P(),
            P(None, ("kvp", "tp")),
            P("tp", "kvp"),
            P(("kvp", "tp")),
            P(None, "tp", "kvp"),
            P(None, "tp", "kvp"),
        ),
        out_specs=(P("kvp", None, None, "tp"), P(None, ("kvp", "tp")), P(None, ("kvp", "tp"))),
        check_vma=False,
    )
```

profile of v0, /device:TPU:8, one launch (start us, length us, event | category | flops | bytes accessed | tf_op | source)
XLA Modules:
  0.0 610.4 jit_solution(5732478433936391505)
XLA Ops:
  8.1 2.0 sort.34
  10.2 1.6 gather_fusion
  12.6 10.6 %all-to-all-start = ((bf16[64,2,8,128]{3,2,1,0:T(8,128)(2,1)}), bf16[64,2,8,128]{3,2,1,0:T(8,128)(2,1)S(1)}, u32[]{:S(2)}, u32[]{:S(2)}) async-start(bf16[64,2,8,128]{3,2,1,0:T(8,128)(2,1)} %broadcast_select_fusion), calls=%async_computation | async-start | bytes 524288 | tf_op jit(solution)/shard_map/all_to_all | solution.py:80
  23.9 51.9 %all_gather.24 = bf16[2,16,16,128]{2,1,0,3:T(8,128)(2,1)S(1)} all-gather(bf16[2,16,16,2]{2,1,0,3:T(8,128)(2,1)S(1)} %copy.110), channel_id=1, replica_groups=mesh['kvp'=64,'tp'=8] {'kvp'}, dimensions={3}, use_global_device_ids=true | all-gather | bytes 133120 | tf_op jit(solution)/shard_map/all_gather | solution.py:75
  75.8 1.1 copy.111
  77.7 6.5 %sort.35 = (s32[4096]{0:T(1024)}, s32[4096]{0:T(1024)}) sort(s32[4096]{0:T(1024)} %param.15, s32[4096]{0:T(1024)S(1)} %iota.21), dimensions={0}, to_apply=%region_2.3 | sort | flops 49152 | bytes 65536 | tf_op jit(solution)/shard_map/jit(argsort)/sort | solution.py:81
  86.3 1.5 gather_fusion.1
  89.3 2.5 fusion.41
  92.8 1.3 fusion.19
  94.2 1.5 copy.116
  95.7 3.1 reshape.282
  98.8 2.4 fusion.9
  101.3 47.4 %all_gather.29 = bf16[2,16,2,1,128]{1,2,3,0,4:T(2,128)(2,1)S(1)} all-gather(bf16[2,16,2,1,2]{1,2,3,0,4:T(2,128)(2,1)S(1)} %copy.120), channel_id=1, replica_groups=mesh['kvp'=64,'tp'=8] {'kvp'}, dimensions={4}, use_global_device_ids=true | all-gather | bytes 16640 | tf_op jit(solution)/shard_map/all_gather | solution.py:76
  149.0 1.6 fusion.42
  152.1 49.4 %all-gather = f32[1024,32]{1,0:T(8,128)S(1)} all-gather(f32[16,32]{1,0:T(8,128)S(1)} %fusion.38), channel_id=2, replica_groups=mesh['kvp'=64,'tp'=8] {'kvp'}, dimensions={0}, use_global_device_ids=true | all-gather | bytes 133120 | tf_op jit(solution)/shard_map/all_gather | solution.py:17
  201.5 47.8 %all_gather.25 = f32[64,16,32]{2,1,0:T(8,128)S(1)} all-gather(f32[1,16,32]{2,1,0:T(8,128)S(1)} %copy.114), channel_id=1, replica_groups=mesh['kvp'=64,'tp'=8] {'kvp'}, dimensions={0}, use_global_device_ids=true | all-gather | bytes 133120 | tf_op jit(solution)/shard_map/all_gather | solution.py:17
  251.2 126.4 %while.19 = (s32[]{:T(128)}, f32[16,32]{1,0:T(8,128)S(1)}, f32[16,32]{1,0:T(8,128)S(1)}, f32[16,32,128]{2,1,0:T(8,128)S(1)}, f32[64,16,32]{2,1,0:T(8,128)}, /*in...) while((s32[]{:T(128)}, f32[16,32]{1,0:T(8,128)S(1)}, ...), condition=%wide.region_8.9_spmd, body=%wide.region_7.8_spmd.sunk | while | flops 199685 | bytes 1331351 | solution.py:23
  251.9 1.0 constant_dynamic-slice_fusion.3
  253.9 1.0 constant_dynamic-slice_fusion.3
  256.0 1.0 constant_dynamic-slice_fusion.3
  258.0 1.0 constant_dynamic-slice_fusion.3
  260.0 1.0 constant_dynamic-slice_fusion.3
  262.0 1.0 constant_dynamic-slice_fusion.3
  264.0 1.0 constant_dynamic-slice_fusion.3
  266.0 1.0 constant_dynamic-slice_fusion.3
  268.0 1.0 constant_dynamic-slice_fusion.3
  270.0 1.0 constant_dynamic-slice_fusion.3
  272.0 1.0 constant_dynamic-slice_fusion.3
  274.0 1.0 constant_dynamic-slice_fusion.3
  276.0 1.0 constant_dynamic-slice_fusion.3
  278.0 1.0 constant_dynamic-slice_fusion.3
  280.0 1.0 constant_dynamic-slice_fusion.3
  282.0 1.0 constant_dynamic-slice_fusion.3
  284.0 1.0 constant_dynamic-slice_fusion.3
  286.0 1.0 constant_dynamic-slice_fusion.3
  288.1 1.0 constant_dynamic-slice_fusion.3
  290.1 1.0 constant_dynamic-slice_fusion.3
  292.1 1.0 constant_dynamic-slice_fusion.3
  294.1 1.0 constant_dynamic-slice_fusion.3
  296.1 1.0 constant_dynamic-slice_fusion.3
  298.1 1.0 constant_dynamic-slice_fusion.3
  300.1 1.0 constant_dynamic-slice_fusion.3
  302.1 1.0 constant_dynamic-slice_fusion.3
  304.1 1.0 constant_dynamic-slice_fusion.3
  306.1 1.0 constant_dynamic-slice_fusion.3
  308.1 1.0 constant_dynamic-slice_fusion.3
  310.1 1.0 constant_dynamic-slice_fusion.3
  312.1 1.0 constant_dynamic-slice_fusion.3
  314.1 1.0 constant_dynamic-slice_fusion.3
  316.1 1.0 constant_dynamic-slice_fusion.3
  318.1 1.0 constant_dynamic-slice_fusion.3
  320.2 1.0 constant_dynamic-slice_fusion.3
  322.2 1.0 constant_dynamic-slice_fusion.3
  330.2 1.0 constant_dynamic-slice_fusion.3
  340.2 1.0 constant_dynamic-slice_fusion.3
  350.2 1.0 constant_dynamic-slice_fusion.3
  358.3 1.0 constant_dynamic-slice_fusion.3
  360.3 1.0 constant_dynamic-slice_fusion.3
  368.3 1.0 constant_dynamic-slice_fusion.3
  380.9 1.3 dynamic-slice
  383.1 109.9 %all-reduce = bf16[2048]{0:T(1024)(128)(2,1)S(1)} all-reduce(bf16[2048]{0:T(1024)(128)(2,1)S(1)} %dynamic-update-slice), channel_id=4, replica_groups=mesh['kvp'=64,'tp'=8] {'kvp'}, use_global_device_ids=true, to_apply=%add | all-reduce | flops 2048 | bytes 8192
  493.0 1.3 dynamic-slice.1
  495.8 66.6 %all_gather.30 = bf16[32,2048]{0,1:T(8,128)(2,1)S(1)} all-gather(bf16[32,32]{0,1:T(8,128)(2,1)S(1)} %copy.131), channel_id=1, replica_groups=mesh['kvp'=64,'tp'=8] {'kvp'}, dimensions={1}, use_global_device_ids=true | all-gather | bytes 133120 | tf_op jit(solution)/shard_map/all_gather | solution.py:152
  564.5 37.0 %all-reduce.4 = (bf16[32,416]{1,0:T(8,128)(2,1)S(1)}, bf16[32,416]{1,0:T(8,128)(2,1)S(1)}, bf16[32,8]{0,1:T(8,128)(2,1)S(1)}) all-reduce(bf16[32,416]{1,0:T(8,128)(2,1)S(1)} %convolution_convert_fusion, bf16[32,416]{1,0:T(8,128)(2,1)S(1)} %convolution_convert_fusion.1, ...), channel_id=8, replica_groups=mesh['kvp'=64,'tp'=8] {'tp'}, use_global_device_ids=true, to_apply=%region_15.16.clone | all-reduce | flops 26880 | bytes 107520
  (250 shorter events, 103.5 us)
Async XLA Ops:
  7.2 555.5 %copy-start = (bf16[64,32,416]{2,1,0:T(8,128)(2,1)S(1)}, bf16[64,32,416]{2,1,0:T(8,128)(2,1)}, u32[]{:S(2)}) copy-start(bf16[64,32,416]{2,1,0:T(8,128)(2,1)} %param.21) | copy-start | bytes 5111812
  7.2 69.7 %copy-start.10 = (s32[16]{0:T(128)S(1)}, s32[16]{0:T(128)}, u32[]{:S(2)}) copy-start(s32[16]{0:T(128)} %param.16) | copy-start | bytes 196
  12.6 75.9 %all-to-all-start = ((bf16[64,2,8,128]{3,2,1,0:T(8,128)(2,1)}), bf16[64,2,8,128]{3,2,1,0:T(8,128)(2,1)S(1)}, u32[]{:S(2)}, u32[]{:S(2)}) async-start(bf16[64,2,8,128]{3,2,1,0:T(8,128)(2,1)} %broadcast_select_fusion), calls=%async_computation | async-start | bytes 524288 | tf_op jit(solution)/shard_map/all_to_all | solution.py:80
  23.2 227.0 %all-gather.5.cloned.1.call-start = ((), (), s32[]{:S(2)}) async-start(), calls=%async_computation.2 | async-start | bytes 17039360 | tf_op jit(solution)/shard_map/all_gather | solution.py:17
  75.8 12.7 %copy-start.1 = (bf16[2,16,16,128]{2,1,0,3:T(8,128)(2,1)}, bf16[2,16,16,128]{2,1,0,3:T(8,128)(2,1)S(1)}, u32[]{:S(2)}) copy-start(bf16[2,16,16,128]{2,1,0,3:T(8,128)(2,1)S(1)} %all_gather.24) | copy-start | bytes 393220
  88.6 0.7 copy-start.3
  94.1 4.7 copy-start.7
  95.7 5.6 copy-start.9
  101.2 393.7 %reduce-scatter.6.cloned.1.call-start = ((), (), s32[]{:S(2)}) async-start(), calls=%async_computation.3 | async-start | bytes 73728
  249.3 0.8 copy-start.5
  378.6 1.2 copy-start.4
  378.7 4.1 copy-start.11
  378.8 116.9 %copy-start.8 = (bf16[32,32]{1,0:T(8,128)(2,1)S(1)}, bf16[32,32]{1,0:T(8,128)(2,1)}, u32[]{:S(2)}) copy-start(bf16[32,32]{1,0:T(8,128)(2,1)} %param.17) | copy-start | bytes 6148
  495.7 68.8 %copy-start.6 = (bf16[32,32]{1,0:T(8,128)(2,1)}, bf16[32,32]{1,0:T(8,128)(2,1)S(1)}, u32[]{:S(2)}) copy-start(bf16[32,32]{1,0:T(8,128)(2,1)S(1)} %add_convert_fusion) | copy-start | bytes 6148
  495.8 67.7 %copy-start.2 = (bf16[64,32,416]{2,1,0:T(8,128)(2,1)S(1)}, bf16[64,32,416]{2,1,0:T(8,128)(2,1)}, u32[]{:S(2)}) copy-start(bf16[64,32,416]{2,1,0:T(8,128)(2,1)} %param.20) | copy-start | bytes 5111812
Sparse Core Ops, SparseCore 0:
  101.3 116.2 all-gather.4
  381.0 42.6 reduce-scatter.5
where the time goes:
time: 616 us; the launch traced here: 610 us
  blocking collectives  410 us (67%)
  local copies, waits for them, and re-layouts  84 us (14%)
  other arithmetic  77.5 us (13%)
  between operations  15.7 us (3%)
  matrix products  10.8 us (2%)
  starting transfers between devices  10.6 us (2%)
    unnamed x2, blocking collectives  147 us
    all_gather x2, blocking collectives, merged(): everything = jax.tree.map(lambda part: lax.all_gather(part, axis), array)  97.2 us
    all_gather x1, blocking collectives, shards(): columns = lax.all_gather(stream, 'kvp', axis=1, tiled=True)  66.6 us
    dynamic_slice x63, local copies, waits for them, and re-layouts, turn(): return combine(so_far, jax.tree.map(lambda part: part[k], everything))  61.9 us
    all_gather x1, blocking collectives, shards(): lax.all_gather(queries, 'kvp', axis=3, tiled=True)  51.9 us
    all_gather x1, blocking collectives, shards(): lax.all_gather(fresh_kv, 'kvp', axis=4, tiled=True)  47.4 us
    add x63, other arithmetic, merge_pair(): sum_a * factor_a + sum_b * factor_b  45 us
    add x63, other arithmetic, merge_pair(): num_a * factor_a[..., None] + num_b * factor_b[..., None]  17.7 us
  transfers between devices with their start and end apart: 3, of which 0 were waited for; matrix products, arithmetic and copies ran while one was open for 3% of the time, Pallas kernels for 0%

commit v1 on v0

v1 whole, which is shorter than its diff:
```python
import jax
import jax.numpy as jnp
from jax import lax
from jax.experimental import pallas as pl
from jax.experimental.pallas import tpu as pltpu
from jax.sharding import PartitionSpec as P

D = 16384
HEADS = 128
KVH = 8
HD = 128
STEPS = 2
ROWS = 16
BATCH = STEPS * ROWS

negative = -1e30
epsilon = 1e-05
bf16 = jnp.bfloat16
f32 = jnp.float32
VMEM = pl.BlockSpec(memory_space=pltpu.VMEM)
SMEM = pl.BlockSpec(memory_space=pltpu.SMEM)
PARAMS = pltpu.CompilerParams(vmem_limit_bytes=48 * 1024 * 1024)


def call(body, name, out_shape, in_specs, *args, scratch=()):
    multiple = isinstance(out_shape, (tuple, list))
    return pl.pallas_call(
        body,
        out_shape=out_shape,
        in_specs=in_specs,
        out_specs=[VMEM] * len(out_shape) if multiple else VMEM,
        scratch_shapes=scratch,
        compiler_params=PARAMS,
        name=name,
    )(*args)


def to_owner_order(owner, pages, out):
    base = lax.axis_index("kvp") * pages.shape[0]

    def one(c, carry):
        out[owner[base + c]] = pages[c]
        return carry

    lax.fori_loop(0, pages.shape[0], one, 0, unroll=8)


def attention(context, gathered, pages, out):
    turned = gathered[...].astype(f32).T
    q = turned[: HEADS // KVH * BATCH].astype(bf16)
    fresh = turned[HEADS // KVH * BATCH :].astype(bf16)
    fresh_k, fresh_v = fresh[:BATCH], fresh[BATCH : 2 * BATCH]
    cache = pages[...].astype(f32)
    keys = cache[:, 0].reshape(-1, HD).astype(bf16)
    values = cache[:, 1].reshape(-1, HD).astype(bf16)
    combos, tokens = q.shape[0], keys.shape[0]
    me = lax.axis_index("kvp")
    scale = HD ** (-0.5)
    nt = (((1,), (1,)), ((), ()))
    scores = lax.dot_general(q, keys, nt, preferred_element_type=f32) * scale
    fresh_scores = lax.dot_general(q, fresh_k, nt, preferred_element_type=f32) * scale

    page_len = tokens // pages.shape[0]
    page = (
        lax.broadcasted_iota(jnp.int32, (1, tokens), 1) // page_len + me * pages.shape[0]
    )
    row = jnp.zeros((1, tokens), jnp.int32)
    end = jnp.int32(0)
    for r in range(ROWS - 1):
        end = end + context[r]
        row = row + (page >= end).astype(jnp.int32)
    combo = lax.broadcasted_iota(jnp.int32, (combos, 1), 0)
    combo_row = combo % ROWS
    combo_step = (combo // ROWS) % STEPS
    member = combo_row == row
    entry = lax.broadcasted_iota(jnp.int32, (1, BATCH), 1)
    fresh_member = (
        (combo_row == entry % ROWS) & (entry // ROWS <= combo_step) & (me == 0)
    )
    scores = jnp.where(member, scores, negative)
    fresh_scores = jnp.where(fresh_member, fresh_scores, negative)
    peak = jnp.maximum(
        jnp.max(scores, axis=1, keepdims=True), jnp.max(fresh_scores, axis=1, keepdims=True)
    )
    peak = peak.astype(bf16).astype(f32)
    weights = jnp.where(member, jnp.exp(scores - peak), 0.0)
    fresh_weights = jnp.where(fresh_member, jnp.exp(fresh_scores - peak), 0.0)
    total = jnp.sum(weights, axis=1, keepdims=True) + jnp.sum(
        fresh_weights, axis=1, keepdims=True
    )
    numerator = jnp.dot(
        weights.astype(bf16), values, preferred_element_type=f32
    ) + jnp.dot(fresh_weights.astype(bf16), fresh_v, preferred_element_type=f32)
    high = total.astype(bf16).astype(f32)
    lane = lax.broadcasted_iota(jnp.int32, (combos, HD), 1)
    stats = jnp.where(lane < 32, peak, jnp.where(lane < 64, high, total - high))
    peers = out.shape[0]
    out[...] = jnp.concatenate(
        [numerator.reshape(peers, -1, HD), stats.reshape(peers, -1, HD)], axis=1
    ).astype(bf16)


def merge(parts, out):
    x = parts[...].astype(f32)
    count = x.shape[1] // 2
    numerator, stats = x[:, :count], x[:, count:]
    peak = stats[:, :, 0:1]
    total = stats[:, :, 32:33] + stats[:, :, 64:65]
    top = jnp.max(peak, axis=0, keepdims=True)
    factor = jnp.exp(peak - top)
    denominator = jnp.sum(factor * total, axis=0)
    value = jnp.sum(factor * numerator, axis=0) / denominator
    out[...] = jnp.broadcast_to(value.astype(bf16)[None], out.shape)


def pack(x):
    return jnp.concatenate([x[8 * q : 8 * q + 8] for q in range(4)], axis=1)


def project(attended, weight, out):
    x = attended[...].astype(f32).reshape(-1, BATCH, HD).astype(bf16)
    flat = jnp.concatenate([x[h] for h in range(x.shape[0])], axis=1)
    acc = jnp.dot(flat, weight[...], preferred_element_type=f32)
    for j in range(out.shape[0]):
        out[j] = pack(acc[:, 32 * j : 32 * j + 32]).astype(bf16)


def add_residual(parts, residual, stream, sent):
    total = jnp.sum(parts[...].astype(f32), axis=0)
    value = (total + pack(residual[...].astype(f32))).astype(bf16)
    sent[...] = jnp.broadcast_to(value[None], sent.shape)
    wide = value.astype(f32)
    stream[...] = jnp.concatenate(
        [wide[:, 32 * q : 32 * q + 32] for q in range(4)], axis=0
    ).astype(bf16)


def feed_forward(columns, gain, gate_weight, up_weight, out):
    x = columns[...].astype(f32)
    square = jnp.sum(x * x, axis=0)
    square = jnp.concatenate(
        [jnp.sum(square[:, 32 * q : 32 * q + 32], axis=1, keepdims=True) for q in range(4)],
        axis=0,
    )
    scaled = (x * gain[...].astype(f32)).reshape(-1, 4, 8, HD)
    lane = lax.broadcasted_iota(jnp.int32, (scaled.shape[0], 8, HD), 2) // 32
    blocks = []
    for q in range(4):
        block = None
        for t in range(4):
            piece = scaled[:, t]
            if t != q:
                piece = pltpu.roll(piece, (t - q) * 32 % HD, 2)
            block = piece if block is None else jnp.where(lane == t, piece, block)
        blocks.append(block)
    rows = jnp.concatenate(blocks, axis=1).astype(bf16)
    flat = jnp.concatenate([rows[g] for g in range(rows.shape[0])], axis=1)
    width = gate_weight.shape[2]
    gate = jnp.dot(flat, gate_weight[...].reshape(-1, width), preferred_element_type=f32)
    up = jnp.dot(flat, up_weight[...].reshape(-1, width), preferred_element_type=f32)
    peers = out.shape[0]
    part = width // peers
    high = square.astype(bf16).astype(f32)
    tail = lax.broadcasted_iota(jnp.int32, (BATCH, 64 - part), 1)
    tail = jnp.where(tail == 0, high, jnp.where(tail == 1, square - high, 0.0))
    gap = jnp.zeros((BATCH, 64 - part), f32)
    for j in range(peers):
        out[j] = jnp.concatenate(
            [
                gate[:, part * j : part * j + part],
                gap,
                up[:, part * j : part * j + part],
                tail,
            ],
            axis=1,
        ).astype(bf16)


def activate(parts, out):
    total = jnp.sum(parts[...].astype(f32), axis=0)
    part = out.shape[1]
    square = total[:, 64 + part : 65 + part] + total[:, 65 + part : 66 + part]
    inverse = lax.rsqrt(square / D + epsilon)
    gated = total[:, :part] * inverse
    lifted = total[:, 64 : 64 + part] * inverse
    out[...] = (gated / (1.0 + jnp.exp(-gated)) * lifted).astype(bf16)


def exchange(x, axis):
    return lax.all_to_all(x, axis, split_axis=0, concat_axis=0, tiled=True)


def shards(
    queries,
    fresh_kv,
    kv_cache,
    page_owner,
    context_pages,
    residual,
    out_proj,
    norm_gain,
    gate_weight,
    up_weight,
):
    kvp = lax.axis_size("kvp")
    tp = lax.axis_size("tp")
    shape = jax.ShapeDtypeStruct
    combos = queries.shape[2] * BATCH

    q = queries.transpose(3, 2, 0, 1).reshape(2, combos)
    fresh = fresh_kv[:, :, :, 0].transpose(3, 2, 0, 1).reshape(2, 2 * BATCH)
    gain = jnp.tile(norm_gain, 4).reshape(2, 2 * BATCH)
    sent = jnp.concatenate([q, fresh, gain], axis=1)
    gathered = exchange(jnp.broadcast_to(sent[None], (kvp,) + sent.shape), "kvp")
    gain_rows = gathered[:, :, combos + 2 * BATCH :].reshape(kvp, 1, HD)

    outgoing = call(
        to_owner_order, "to_owner_order", shape(kv_cache.shape, bf16), [SMEM, VMEM], page_owner, kv_cache
    )
    parts = call(
        attention,
        "attention",
        shape((kvp, 2 * combos // kvp, HD), bf16),
        [SMEM, VMEM, VMEM],
        context_pages,
        gathered.reshape(2 * kvp, -1),
        kv_cache,
    )
    parts = exchange(parts, "kvp")
    piece = call(merge, "merge", shape((kvp, combos // kvp, HD), bf16), [VMEM], parts)
    attended = exchange(piece, "kvp")
    partial = call(
        project, "project", shape((tp, 8, HD), bf16), [VMEM, VMEM], attended, out_proj
    )
    partial, outgoing = lax.optimization_barrier((partial, outgoing))
    regrouped = exchange(outgoing, "kvp")
    summands = exchange(partial, "tp")
    stream, block = call(
        add_residual,
        "add_residual",
        [shape(residual.shape, bf16), shape((kvp, 8, HD), bf16)],
        [VMEM, VMEM],
        summands,
        residual,
    )
    columns = exchange(block, "kvp")
    lifted = call(
        feed_forward,
        "feed_forward",
        shape((tp, BATCH, HD), bf16),
        [VMEM] * 4,
        columns,
        gain_rows,
        gate_weight,
        up_weight,
    )
    lifted = exchange(lifted, "tp")
    hidden = call(
        activate, "activate", shape((BATCH, gate_weight.shape[2] // tp), bf16), [VMEM], lifted
    )
    return regrouped, stream, hidden


def solution(mesh):
    return jax.shard_map(
        shards,
        mesh=mesh,
        in_specs=(
            P(None, None, "tp", "kvp"),
            P(None, None, None, "tp", "kvp"),
            P("kvp", None, None, "tp"),
            P(),
            P(),
            P(None, ("kvp", "tp")),
            P("tp", "kvp"),
            P(("kvp", "tp")),
            P(None, "tp", "kvp"),
            P(None, "tp", "kvp"),
        ),
        out_specs=(P("kvp", None, None, "tp"), P(None, ("kvp", "tp")), P(None, ("kvp", "tp"))),
        check_vma=False,
    )
```

time: 616 us -> 131 us (0.21)
  the two profiles are of different devices: /device:TPU:8 before, /device:TPU:1 now
where the time goes in v1:
time: 131 us
  blocking collectives  66.2 us (51%)
  waiting for transfers between devices  31.4 us (24%)
  starting transfers between devices  16.3 us (12%)
  local copies, waits for them, and re-layouts  9.18 us (7%)
  Pallas kernels  6.97 us (5%)
    all_to_all x4, blocking collectives, exchange(): return lax.all_to_all(x, axis, split_axis=0, concat_axis=0, tiled=True)  66.2 us
    all_to_all x3, waiting for transfers between devices, exchange(): return lax.all_to_all(x, axis, split_axis=0, concat_axis=0, tiled=True)  31.4 us
    all_to_all x3, starting transfers between devices, exchange(): return lax.all_to_all(x, axis, split_axis=0, concat_axis=0, tiled=True)  16.3 us
    pallas_call x7, Pallas kernels, call(): pl.pallas_call(body, out_shape=out_shape, in_specs=in_specs, out_specs=[V...  6.97 us
    unnamed x17, local copies, waits for them, and re-layouts  6.26 us
  transfers between devices with their start and end apart: 3, of which 3 were waited for; matrix products, arithmetic and copies ran while one was open for 0% of the time, Pallas kernels for 2%

profile of v1, /device:TPU:1, one launch (start us, length us, event | category | flops | bytes accessed | tf_op | source)
XLA Modules:
  0.0 130.7 jit_solution(9866711752784061477)
XLA Ops:
  0.6 0.0 copy-start.2
  0.6 0.7 tile.10
  1.4 0.1 reshape.26
  1.5 0.7 copy.15
  2.2 0.1 reshape.22
  2.2 0.8 copy.14
  3.1 0.1 reshape.21
  3.1 0.1 pad.2.clone
  3.2 0.1 broadcast_in_dim.2
  3.3 23.1 %all_to_all.35 = bf16[64,2,640]{2,1,0:T(2,128)(2,1)S(1)} all-to-all(bf16[64,2,640]{2,1,0:T(2,128)(2,1)S(1)} %broadcast_in_dim.2), channel_id=1, replica_groups=mesh['kvp'=64,'tp'=8] {'kvp'}, dimensions={0} | all-to-all | bytes 327680 | tf_op jit(solution)/shard_map/all_to_all | solution.py:190
  26.4 0.1 reshape.23.gathered
  26.5 0.0 copy-start.3
  26.5 0.9 copy-done.3
  27.5 0.0 copy-start.7
  27.5 0.7 copy-done.7
  28.1 0.0 copy-start
  28.1 1.5 %attention.1 = bf16[64,16,128]{2,1,0:T(8,128)(2,1)S(1)} custom-call(s32[16]{0:T(128)S(1)} %copy-done.7, bf16[128,640]{1,0:T(8,128)(2,1)S(1)} %reshape.23.gathered, bf16[64,2,8,128]{3,2,1,0:T(8,128)(2,1)S(1)} %copy-done.3), custom_call_target="tpu_custom_call" | custom-call | tf_op jit(solution)/shard_map/attention/pallas_call | solution.py:27
  29.6 17.1 %all_to_all.36.parts = bf16[64,16,128]{2,1,0:T(8,128)(2,1)S(1)} all-to-all(bf16[64,16,128]{2,1,0:T(8,128)(2,1)S(1)} %attention.1), channel_id=1, replica_groups=mesh['kvp'=64,'tp'=8] {'kvp'}, dimensions={0} | all-to-all | bytes 524288 | tf_op jit(solution)/shard_map/all_to_all | solution.py:190
  46.7 0.9 merge.1
  47.6 4.7 %all-to-all-start.2 = ((bf16[64,8,128]{2,1,0:T(8,128)(2,1)}), bf16[64,8,128]{2,1,0:T(8,128)(2,1)S(1)}, u32[]{:S(2)}, u32[]{:S(2)}) async-start(bf16[64,8,128]{2,1,0:T(8,128)(2,1)} %merge.1), calls=%async_computation.2 | async-start | bytes 262144 | tf_op jit(solution)/shard_map/all_to_all | solution.py:190
  52.3 0.0 copy-start.4
  52.4 0.9 copy-done.4
  53.3 0.0 copy-start.5
  53.3 0.7 copy-done.5
  54.0 1.6 %to_owner_order.1 = bf16[64,2,8,128]{3,2,1,0:T(8,128)(2,1)} custom-call(s32[4096]{0:T(1024)S(1)} %copy-done.5, bf16[64,2,8,128]{3,2,1,0:T(8,128)(2,1)S(1)} %copy-done.4), custom_call_target="tpu_custom_call" | custom-call | tf_op jit(solution)/shard_map/to_owner_order/pallas_call | solution.py:27
  55.7 7.8 %all-to-all-done.2.attended = bf16[64,8,128]{2,1,0:T(8,128)(2,1)S(1)} async-done(((bf16[64,8,128]{2,1,0:T(8,128)(2,1)}), bf16[64,8,128]{2,1,0:T(8,128)(2,1)S(1)}, u32[]{:S(2)}, u32[]{:S(2)}) %all-to-all-start.2) | async-done | bytes 131104 | tf_op jit(solution)/shard_map/all_to_all | solution.py:190
  63.5 0.0 copy-done.2
  63.5 0.4 project.1
  63.8 16.5 %all_to_all.37.parts = bf16[8,8,128]{2,1,0:T(8,128)(2,1)S(1)} all-to-all(bf16[8,8,128]{2,1,0:T(8,128)(2,1)S(1)} %project.1), channel_id=1, replica_groups=mesh['kvp'=64,'tp'=8] {'tp'}, dimensions={0} | all-to-all | bytes 32768 | tf_op jit(solution)/shard_map/all_to_all | solution.py:190
  80.3 0.0 copy-start.6
  80.3 0.7 copy-done.6
  81.0 0.7 add_residual.1
  81.7 5.9 %all-to-all-start.5 = ((bf16[64,8,128]{2,1,0:T(8,128)(2,1)}), bf16[64,8,128]{2,1,0:T(8,128)(2,1)S(1)}, u32[]{:S(2)}, u32[]{:S(2)}) async-start(bf16[64,8,128]{2,1,0:T(8,128)(2,1)} %get-tuple-element.10), calls=%async_computation.5 | async-start | bytes 262144 | tf_op jit(solution)/shard_map/all_to_all | solution.py:190
  87.6 0.1 slice.4
  87.7 0.1 reshape.25.gain
  87.8 11.1 %all-to-all-done.5.columns = bf16[64,8,128]{2,1,0:T(8,128)(2,1)S(1)} async-done(((bf16[64,8,128]{2,1,0:T(8,128)(2,1)}), bf16[64,8,128]{2,1,0:T(8,128)(2,1)S(1)}, u32[]{:S(2)}, u32[]{:S(2)}) %all-to-all-start.5) | async-done | bytes 131104 | tf_op jit(solution)/shard_map/all_to_all | solution.py:190
  99.0 0.0 copy-done
  99.0 0.0 copy-start.1
  99.0 1.6 %copy-done.1 = bf16[64,32,416]{2,1,0:T(8,128)(2,1)S(1)} copy-done((bf16[64,32,416]{2,1,0:T(8,128)(2,1)S(1)}, bf16[64,32,416]{2,1,0:T(8,128)(2,1)}, u32[]{:S(2)}) %copy-start.1) | copy-done | bytes 1703960
  100.5 1.0 feed_forward.1
  101.5 9.5 %all_to_all.38.parts = bf16[8,32,128]{2,1,0:T(8,128)(2,1)S(1)} all-to-all(bf16[8,32,128]{2,1,0:T(8,128)(2,1)S(1)} %feed_forward.1), channel_id=1, replica_groups=mesh['kvp'=64,'tp'=8] {'tp'}, dimensions={0} | all-to-all | bytes 131072 | tf_op jit(solution)/shard_map/all_to_all | solution.py:190
  111.0 5.7 %all-to-all-start.3 = ((bf16[64,2,8,128]{3,2,1,0:T(8,128)(2,1)}), bf16[64,2,8,128]{3,2,1,0:T(8,128)(2,1)S(1)}, u32[]{:S(2)}, u32[]{:S(2)}) async-start(bf16[64,2,8,128]{3,2,1,0:T(8,128)(2,1)} %to_owner_order.1), calls=%async_computation.3 | async-start | bytes 524288 | tf_op jit(solution)/shard_map/all_to_all | solution.py:190
  116.7 0.8 activate.1
  117.6 12.4 %all-to-all-done.3 = bf16[64,2,8,128]{3,2,1,0:T(8,128)(2,1)S(1)} async-done(((bf16[64,2,8,128]{3,2,1,0:T(8,128)(2,1)}), bf16[64,2,8,128]{3,2,1,0:T(8,128)(2,1)S(1)}, u32[]{:S(2)}, u32[]{:S(2)}) %all-to-all-start.3) | async-done | bytes 262176 | tf_op jit(solution)/shard_map/all_to_all | solution.py:190
  130.0 0.7 copy.18
  (1 shorter events, 0.0 us)
Async XLA Ops:
  0.6 62.8 %copy-start.2 = (bf16[2048,256]{1,0:T(8,128)(2,1)S(1)}, bf16[2048,256]{1,0:T(8,128)(2,1)}, u32[]{:S(2)}) copy-start(bf16[2048,256]{1,0:T(8,128)(2,1)} %weight.1) | copy-start | bytes 3145732
  26.5 1.0 copy-start.3
  27.5 0.7 copy-start.7
  28.1 70.8 %copy-start = (bf16[64,32,416]{2,1,0:T(8,128)(2,1)S(1)}, bf16[64,32,416]{2,1,0:T(8,128)(2,1)}, u32[]{:S(2)}) copy-start(bf16[64,32,416]{2,1,0:T(8,128)(2,1)} %gate_weight.1) | copy-start | bytes 5111812
  47.6 15.8 %all-to-all-start.2 = ((bf16[64,8,128]{2,1,0:T(8,128)(2,1)}), bf16[64,8,128]{2,1,0:T(8,128)(2,1)S(1)}, u32[]{:S(2)}, u32[]{:S(2)}) async-start(bf16[64,8,128]{2,1,0:T(8,128)(2,1)} %merge.1), calls=%async_computation.2 | async-start | bytes 262144 | tf_op jit(solution)/shard_map/all_to_all | solution.py:190
  52.3 1.0 copy-start.4
  53.3 0.7 copy-start.5
  80.3 0.7 copy-start.6
  81.7 17.2 %all-to-all-start.5 = ((bf16[64,8,128]{2,1,0:T(8,128)(2,1)}), bf16[64,8,128]{2,1,0:T(8,128)(2,1)S(1)}, u32[]{:S(2)}, u32[]{:S(2)}) async-start(bf16[64,8,128]{2,1,0:T(8,128)(2,1)} %get-tuple-element.10), calls=%async_computation.5 | async-start | bytes 262144 | tf_op jit(solution)/shard_map/all_to_all | solution.py:190
  99.0 1.6 %copy-start.1 = (bf16[64,32,416]{2,1,0:T(8,128)(2,1)S(1)}, bf16[64,32,416]{2,1,0:T(8,128)(2,1)}, u32[]{:S(2)}) copy-start(bf16[64,32,416]{2,1,0:T(8,128)(2,1)} %up_weight.1) | copy-start | bytes 5111812
  111.0 18.9 %all-to-all-start.3 = ((bf16[64,2,8,128]{3,2,1,0:T(8,128)(2,1)}), bf16[64,2,8,128]{3,2,1,0:T(8,128)(2,1)S(1)}, u32[]{:S(2)}, u32[]{:S(2)}) async-start(bf16[64,2,8,128]{3,2,1,0:T(8,128)(2,1)} %to_owner_order.1), calls=%async_computation.3 | async-start | bytes 524288 | tf_op jit(solution)/shard_map/all_to_all | solution.py:190

commit v2 on v1

--- a/solution.py
+++ b/solution.py
@@ -19,56 +19,102 @@
 f32 = jnp.float32
 VMEM = pl.BlockSpec(memory_space=pltpu.VMEM)
 SMEM = pl.BlockSpec(memory_space=pltpu.SMEM)
-PARAMS = pltpu.CompilerParams(vmem_limit_bytes=48 * 1024 * 1024)
-
-
-def call(body, name, out_shape, in_specs, *args, scratch=()):
-    multiple = isinstance(out_shape, (tuple, list))
+PARAMS = pltpu.CompilerParams(vmem_limit_bytes=16 * 1024 * 1024)
+HBM = pl.BlockSpec(memory_space=pltpu.HBM)
+
+
+def call(body, name, out_shape, in_specs, *args, out_specs=None, scratch=()):
+    if out_specs is None:
+        out_specs = [VMEM] * len(out_shape) if isinstance(out_shape, list) else VMEM
     return pl.pallas_call(
         body,
         out_shape=out_shape,
         in_specs=in_specs,
-        out_specs=[VMEM] * len(out_shape) if multiple else VMEM,
+        out_specs=out_specs,
         scratch_shapes=scratch,
         compiler_params=PARAMS,
         name=name,
     )(*args)
 
 
-def to_owner_order(owner, pages, out):
-    base = lax.axis_index("kvp") * pages.shape[0]
+def pack_inputs(raw, out):
+    heads = raw.shape[3]
+    blocks = raw[...].astype(f32)
+    rows = blocks[:, :ROWS].reshape(2 * BATCH, heads).astype(bf16)
+    entry = lax.broadcasted_iota(jnp.int32, (2 * BATCH, heads * BATCH), 0)
+    target = lax.broadcasted_iota(jnp.int32, (2 * BATCH, heads * BATCH), 1)
+    head = lax.broadcasted_iota(jnp.int32, (heads, heads * BATCH), 0)
+    lane = lax.broadcasted_iota(jnp.int32, (heads, heads * BATCH), 1)
+    lines = []
+    for d in range(2):
+        place = (entry % 2 == d) & (entry // 2 == target % BATCH)
+        spread = lax.dot_general(
+            rows,
+            jnp.where(place, 1.0, 0.0).astype(bf16),
+            (((0,), (0,)), ((), ())),
+            preferred_element_type=f32,
+        )
+        lines.append(
+            jnp.sum(jnp.where(lane // BATCH == head, spread, 0.0), axis=0, keepdims=True)
+        )
+    q = jnp.concatenate(lines, axis=0)
+    kv = [blocks[u, ROWS + w] for w in range(2) for u in range(STEPS)]
+    g = blocks[0, ROWS + 2]
+    g = jnp.concatenate([g[:1], g[1:]] * 2, axis=1)
+    line = jnp.concatenate([q] + kv + [jnp.concatenate([g, g], axis=0)], axis=1)
+    out[...] = jnp.broadcast_to(line.astype(bf16)[None], out.shape)
+
+
+def prepare(context, owner, pages, residual, keys, values, row_of, ordered, packed):
+    me = lax.axis_index("kvp")
+    count, page_len = pages.shape[0], pages.shape[2]
+    cache = pages[...].astype(f32)
+    keys[...] = cache[:, 0].reshape(-1, HD).astype(bf16)
+    values[...] = cache[:, 1].reshape(-1, HD).astype(bf16)
+    page = lax.broadcasted_iota(jnp.int32, row_of.shape, 1) // page_len + me * count
+    row = jnp.zeros(row_of.shape, jnp.int32)
+    end = jnp.int32(0)
+    for r in range(ROWS - 1):
+        end = end + context[r]
+        row = row + (page >= end).astype(jnp.int32)
+    row_of[...] = row
+    packed[...] = pack(residual[...].astype(f32))
 
     def one(c, carry):
-        out[owner[base + c]] = pages[c]
+        ordered[owner[me * count + c]] = pages[c].reshape(2 * page_len, HD)
         return carry
 
-    lax.fori_loop(0, pages.shape[0], one, 0, unroll=8)
-
-
-def attention(context, gathered, pages, out):
+    lax.fori_loop(0, count, one, 0, unroll=8)
+
+
+def attention(gathered, key_ref, value_ref, row_ref, out, gain_out):
     turned = gathered[...].astype(f32).T
     q = turned[: HEADS // KVH * BATCH].astype(bf16)
     fresh = turned[HEADS // KVH * BATCH :].astype(bf16)
     fresh_k, fresh_v = fresh[:BATCH], fresh[BATCH : 2 * BATCH]
-    cache = pages[...].astype(f32)
-    keys = cache[:, 0].reshape(-1, HD).astype(bf16)
-    values = cache[:, 1].reshape(-1, HD).astype(bf16)
+    keys, values = key_ref[...], value_ref[...]
     combos, tokens = q.shape[0], keys.shape[0]
+    peers = out.shape[0]
+    tail = gathered[...][:, combos + 2 * BATCH :]
+    take = lax.broadcasted_iota(jnp.int32, (peers, 2 * peers), 1) - 2 * lax.broadcasted_iota(
+        jnp.int32, (peers, 2 * peers), 0
+    )
+    gain_out[...] = jnp.concatenate(
+        [
+            jnp.dot(
+                jnp.where(take == k, 1.0, 0.0).astype(bf16), tail, preferred_element_type=f32
+            )
+            for k in range(2)
+        ],
+        axis=1,
+    )
     me = lax.axis_index("kvp")
     scale = HD ** (-0.5)
     nt = (((1,), (1,)), ((), ()))
     scores = lax.dot_general(q, keys, nt, preferred_element_type=f32) * scale
     fresh_scores = lax.dot_general(q, fresh_k, nt, preferred_element_type=f32) * scale
 
-    page_len = tokens // pages.shape[0]
-    page = (
-        lax.broadcasted_iota(jnp.int32, (1, tokens), 1) // page_len + me * pages.shape[0]
-    )
-    row = jnp.zeros((1, tokens), jnp.int32)
-    end = jnp.int32(0)
-    for r in range(ROWS - 1):
-        end = end + context[r]
-        row = row + (page >= end).astype(jnp.int32)
+    row = row_ref[...][:1]
     combo = lax.broadcasted_iota(jnp.int32, (combos, 1), 0)
     combo_row = combo % ROWS
     combo_step = (combo // ROWS) % STEPS
@@ -94,13 +140,12 @@
     high = total.astype(bf16).astype(f32)
     lane = lax.broadcasted_iota(jnp.int32, (combos, HD), 1)
     stats = jnp.where(lane < 32, peak, jnp.where(lane < 64, high, total - high))
-    peers = out.shape[0]
     out[...] = jnp.concatenate(
         [numerator.reshape(peers, -1, HD), stats.reshape(peers, -1, HD)], axis=1
     ).astype(bf16)
 
 
-def merge(parts, out):
+def merge(parts, ordered, out):
     x = parts[...].astype(f32)
     count = x.shape[1] // 2
     numerator, stats = x[:, :count], x[:, count:]
@@ -110,7 +155,8 @@
     factor = jnp.exp(peak - top)
     denominator = jnp.sum(factor * total, axis=0)
     value = jnp.sum(factor * numerator, axis=0) / denominator
-    out[...] = jnp.broadcast_to(value.astype(bf16)[None], out.shape)
+    value = jnp.broadcast_to(value.astype(bf16)[None], (out.shape[0],) + value.shape)
+    out[...] = jnp.concatenate([ordered[...], value], axis=1)
 
 
 def pack(x):
@@ -118,31 +164,40 @@
 
 
 def project(attended, weight, out):
-    x = attended[...].astype(f32).reshape(-1, BATCH, HD).astype(bf16)
+    x = attended[...][:, 16:].astype(f32).reshape(-1, BATCH, HD).astype(bf16)
     flat = jnp.concatenate([x[h] for h in range(x.shape[0])], axis=1)
     acc = jnp.dot(flat, weight[...], preferred_element_type=f32)
     for j in range(out.shape[0]):
         out[j] = pack(acc[:, 32 * j : 32 * j + 32]).astype(bf16)
 
 
-def add_residual(parts, residual, stream, sent):
+def add_residual(parts, residual, own, sent):
     total = jnp.sum(parts[...].astype(f32), axis=0)
-    value = (total + pack(residual[...].astype(f32))).astype(bf16)
+    value = (total + residual[...]).astype(bf16)
+    own[...] = value.astype(f32)
     sent[...] = jnp.broadcast_to(value[None], sent.shape)
-    wide = value.astype(f32)
-    stream[...] = jnp.concatenate(
+
+
+def feed_forward(
+    columns, gain, gate_weight, up_weight, own, pages, out, stream, regrouped, staged, done
+):
+    wide = own[...]
+    staged[...] = jnp.concatenate(
         [wide[:, 32 * q : 32 * q + 32] for q in range(4)], axis=0
     ).astype(bf16)
-
-
-def feed_forward(columns, gain, gate_weight, up_weight, out):
+    copies = [
+        pltpu.make_async_copy(pages.at[:, : regrouped.shape[1]], regrouped, done.at[0]),
+        pltpu.make_async_copy(staged, stream, done.at[1]),
+    ]
+    for copy in copies:
+        copy.start()
     x = columns[...].astype(f32)
     square = jnp.sum(x * x, axis=0)
     square = jnp.concatenate(
         [jnp.sum(square[:, 32 * q : 32 * q + 32], axis=1, keepdims=True) for q in range(4)],
         axis=0,
     )
-    scaled = (x * gain[...].astype(f32)).reshape(-1, 4, 8, HD)
+    scaled = (x * gain[...][:, None, :]).reshape(-1, 4, 8, HD)
     lane = lax.broadcasted_iota(jnp.int32, (scaled.shape[0], 8, HD), 2) // 32
     blocks = []
     for q in range(4):
@@ -174,6 +229,8 @@
             ],
             axis=1,
         ).astype(bf16)
+    for copy in copies:
+        copy.wait()
 
 
 def activate(parts, out):
@@ -207,58 +264,96 @@
     shape = jax.ShapeDtypeStruct
     combos = queries.shape[2] * BATCH
 
-    q = queries.transpose(3, 2, 0, 1).reshape(2, combos)
-    fresh = fresh_kv[:, :, :, 0].transpose(3, 2, 0, 1).reshape(2, 2 * BATCH)
-    gain = jnp.tile(norm_gain, 4).reshape(2, 2 * BATCH)
-    sent = jnp.concatenate([q, fresh, gain], axis=1)
-    gathered = exchange(jnp.broadcast_to(sent[None], (kvp,) + sent.shape), "kvp")
-    gain_rows = gathered[:, :, combos + 2 * BATCH :].reshape(kvp, 1, HD)
-
-    outgoing = call(
-        to_owner_order, "to_owner_order", shape(kv_cache.shape, bf16), [SMEM, VMEM], page_owner, kv_cache
-    )
-    parts = call(
+    count, page_len = kv_cache.shape[0], kv_cache.shape[2]
+    tokens = count * page_len
+    raw = jnp.concatenate(
+        [
+            queries.transpose(0, 1, 3, 2),
+            fresh_kv[:, :, :, 0].transpose(0, 2, 3, 1),
+            jnp.broadcast_to(norm_gain.reshape(1, 1, 2, ROWS), (STEPS, 1, 2, ROWS)),
+        ],
+        axis=1,
+    )
+    sent = call(
+        pack_inputs,
+        "pack_inputs",
+        shape((kvp, 2, combos + 4 * BATCH), bf16),
+        [VMEM],
+        raw,
+    )
+    gathered = exchange(sent, "kvp")
+    keys, values, row_of, ordered, packed = call(
+        prepare,
+        "prepare",
+        [
+            shape((tokens, HD), bf16),
+            shape((tokens, HD), bf16),
+            shape((8, tokens), jnp.int32),
+            shape((count, 2 * page_len, HD), bf16),
+            shape((8, HD), f32),
+        ],
+        [SMEM, SMEM, VMEM, VMEM],
+        context_pages,
+        page_owner,
+        kv_cache,
+        residual,
+    )
+    parts, gain_rows = call(
         attention,
         "attention",
-        shape((kvp, 2 * combos // kvp, HD), bf16),
-        [SMEM, VMEM, VMEM],
-        context_pages,
+        [shape((kvp, 2 * combos // kvp, HD), bf16), shape((kvp, HD), f32)],
+        [VMEM] * 4,
         gathered.reshape(2 * kvp, -1),
-        kv_cache,
+        keys,
+        values,
+        row_of,
     )
     parts = exchange(parts, "kvp")
-    piece = call(merge, "merge", shape((kvp, combos // kvp, HD), bf16), [VMEM], parts)
+    piece = call(
+        merge,
+        "merge",
+        shape((kvp, 2 * page_len + combos // kvp, HD), bf16),
+        [VMEM] * 2,
+        parts,
+        ordered,
+    )
     attended = exchange(piece, "kvp")
     partial = call(
         project, "project", shape((tp, 8, HD), bf16), [VMEM, VMEM], attended, out_proj
     )
-    partial, outgoing = lax.optimization_barrier((partial, outgoing))
-    regrouped = exchange(outgoing, "kvp")
     summands = exchange(partial, "tp")
-    stream, block = call(
+    own, block = call(
         add_residual,
         "add_residual",
-        [shape(residual.shape, bf16), shape((kvp, 8, HD), bf16)],
+        [shape((8, HD), f32), shape((kvp, 8, HD), bf16)],
         [VMEM, VMEM],
         summands,
-        residual,
+        packed,
     )
     columns = exchange(block, "kvp")
-    lifted = call(
+    lifted, stream, regrouped = call(
         feed_forward,
         "feed_forward",
-        shape((tp, BATCH, HD), bf16),
-        [VMEM] * 4,
+        [
+            shape((tp, BATCH, HD), bf16),
+            shape(residual.shape, bf16),
+            shape((count, 2 * page_len, HD), bf16),
+        ],
+        [VMEM] * 6,
         columns,
         gain_rows,
         gate_weight,
         up_weight,
+        own,
+        attended,
+        out_specs=[VMEM, HBM, HBM],
+        scratch=[pltpu.VMEM(residual.shape, bf16), pltpu.SemaphoreType.DMA((2,))],
     )
     lifted = exchange(lifted, "tp")
     hidden = call(
         activate, "activate", shape((BATCH, gate_weight.shape[2] // tp), bf16), [VMEM], lifted
     )
-    return regrouped, stream, hidden
+    return regrouped.reshape(kv_cache.shape), stream, hidden
 
 
 def solution(mesh):

time: 131 us -> 112 us (0.85)
  waiting for transfers between devices: 31.4 us -> 7.66 us
  blocking collectives: 66.2 us -> 80.7 us
  local copies, waits for them, and re-layouts: 9.18 us -> 3.92 us
  starting transfers between devices: 16.3 us -> 11.6 us
    all_to_all x3 -> x1, waiting for transfers between devices: 31.4 us -> 7.66 us  [exchange(): return lax.all_to_all(x, axis, split_axis=0, concat_axis=0, tiled=True)]
    all_to_all x4 -> x5, blocking collectives: 66.2 us -> 80.7 us  [exchange(): return lax.all_to_all(x, axis, split_axis=0, concat_axis=0, tiled=True)]
    all_to_all x3 -> x1, starting transfers between devices: 16.3 us -> 11.6 us  [exchange(): return lax.all_to_all(x, axis, split_axis=0, concat_axis=0, tiled=True)]
    unnamed x17 -> x14, local copies, waits for them, and re-layouts: 6.26 us -> 3.03 us
    transpose x2 -> x0, local copies, waits for them, and re-layouts: 1.49 us -> none  [the longest x1 0.81 us: shards(): q = queries.transpose(3, 2, 0, 1).reshape(2, combos)]
    pallas_call x7 -> x8, Pallas kernels: 6.97 us -> 5.98 us  [call(): pl.pallas_call(body, out_shape=out_shape, in_specs=in_specs, out_specs=ou...]
  transfers between devices with their start and end apart: 3 -> 1, of which waited for: 3 -> 1; matrix products, arithmetic and copies ran while one was open for 0% -> 0% of each run, Pallas kernels for 2% -> 1%
where the time goes in v2:
time: 112 us; the launch traced here: 111 us
  blocking collectives  80.7 us (72%)
  starting transfers between devices  11.6 us (10%)
  waiting for transfers between devices  7.66 us (7%)
  Pallas kernels  5.98 us (5%)
  local copies, waits for them, and re-layouts  3.92 us (4%)
    all_to_all x5, blocking collectives, exchange(): return lax.all_to_all(x, axis, split_axis=0, concat_axis=0, tiled=True)  80.7 us
    all_to_all x1, starting transfers between devices, exchange(): return lax.all_to_all(x, axis, split_axis=0, concat_axis=0, tiled=True)  11.6 us
    all_to_all x1, waiting for transfers between devices, exchange(): return lax.all_to_all(x, axis, split_axis=0, concat_axis=0, tiled=True)  7.66 us
    pallas_call x8, Pallas kernels, call(): pl.pallas_call(body, out_shape=out_shape, in_specs=in_specs, out_specs=ou...  5.98 us
    unnamed x14, local copies, waits for them, and re-layouts  3.03 us
  transfers between devices with their start and end apart: 1, of which 1 were waited for; matrix products, arithmetic and copies ran while one was open for 0% of the time, Pallas kernels for 1%

profile of v2, /device:TPU:1, one launch (start us, length us, event | category | flops | bytes accessed | tf_op | source)
XLA Modules:
  0.0 111.4 jit_solution(2460263864800173649)
XLA Ops:
  0.6 0.0 copy-start.2
  0.6 0.8 broadcast_in_dim.7
  1.5 0.8 pad_maximum_fusion.raw
  2.2 0.9 pack_inputs.1
  3.1 11.6 %all-to-all-start = ((bf16[64,2,640]{2,1,0:T(2,128)(2,1)}), bf16[64,2,640]{2,1,0:T(2,128)(2,1)S(1)}, u32[]{:S(2)}, u32[]{:S(2)}) async-start(bf16[64,2,640]{2,1,0:T(2,128)(2,1)} %pack_inputs.1), calls=%async_computation | async-start | bytes 327680 | tf_op jit(solution)/shard_map/all_to_all | solution.py:247
  14.8 0.0 copy-start.3
  14.8 0.9 copy-done.3
  15.7 0.0 copy-start.4
  15.7 0.7 copy-done.4
  16.4 0.0 copy-start.5
  16.4 0.7 copy-done.5
  17.1 0.0 copy-start.6
  17.1 0.7 copy-done.6
  17.8 1.0 prepare.1
  18.8 7.7 %all-to-all-done = bf16[64,2,640]{2,1,0:T(2,128)(2,1)S(1)} async-done(((bf16[64,2,640]{2,1,0:T(2,128)(2,1)}), bf16[64,2,640]{2,1,0:T(2,128)(2,1)S(1)}, u32[]{:S(2)}, u32[]{:S(2)}) %all-to-all-start) | async-done | bytes 163872 | tf_op jit(solution)/shard_map/all_to_all | solution.py:247
  26.4 0.1 reshape.16.gathered
  26.5 0.0 copy-start.1
  26.5 1.0 attention.1
  27.6 0.0 copy-start
  27.6 17.2 %all_to_all.30.parts = bf16[64,16,128]{2,1,0:T(8,128)(2,1)S(1)} all-to-all(bf16[64,16,128]{2,1,0:T(8,128)(2,1)S(1)} %get-tuple-element.18), channel_id=1, replica_groups=mesh['kvp'=64,'tp'=8] {'kvp'}, dimensions={0} | all-to-all | bytes 524288 | tf_op jit(solution)/shard_map/all_to_all | solution.py:247
  44.8 0.3 merge.1
  45.1 19.6 %all_to_all.31.attended.pages = bf16[64,24,128]{2,1,0:T(8,128)(2,1)S(1)} all-to-all(bf16[64,24,128]{2,1,0:T(8,128)(2,1)S(1)} %merge.1), channel_id=1, replica_groups=mesh['kvp'=64,'tp'=8] {'kvp'}, dimensions={0} | all-to-all | bytes 786432 | tf_op jit(solution)/shard_map/all_to_all | solution.py:247
  64.6 0.0 copy-done.2
  64.7 0.4 project.1
  65.0 16.5 %all_to_all.32.parts = bf16[8,8,128]{2,1,0:T(8,128)(2,1)S(1)} all-to-all(bf16[8,8,128]{2,1,0:T(8,128)(2,1)S(1)} %project.1), channel_id=1, replica_groups=mesh['kvp'=64,'tp'=8] {'tp'}, dimensions={0} | all-to-all | bytes 32768 | tf_op jit(solution)/shard_map/all_to_all | solution.py:247
  81.5 17.9 %all_to_all.33.columns = bf16[64,8,128]{2,1,0:T(8,128)(2,1)S(1)} all-to-all(bf16[64,8,128]{2,1,0:T(8,128)(2,1)S(1)} %get-tuple-element.21), channel_id=1, replica_groups=mesh['kvp'=64,'tp'=8] {'kvp'}, dimensions={0} | all-to-all | bytes 262144 | tf_op jit(solution)/shard_map/all_to_all | solution.py:247
  99.4 0.0 copy-done.1
  99.4 0.0 copy-done
  99.5 1.6 %feed_forward.1 = (bf16[8,32,128]{2,1,0:T(8,128)(2,1)S(1)}, bf16[32,32]{1,0:T(8,128)(2,1)}, bf16[64,16,128]{2,1,0:T(8,128)(2,1)}) custom-call(bf16[64,8,128]{2,1,0:T(8,128)(2,1)S(1)} %all_to_all.33.columns, f32[64,128]{1,0:T(8,128)S(1)} %get-tuple-element.22.gain, bf16[64,32,416]{2,1,0:T(8,128)(2,1)S(1)} %copy-done, bf16[64,32,416]{2,1,0:T(8,128)(2,1)S(1)} %copy-done.1, ...), custom_call_target="tpu_custom_call" | custom-call | tf_op jit(solution)/shard_map/feed_forward/pallas_call | solution.py:29
  101.0 9.5 %all_to_all.34.parts = bf16[8,32,128]{2,1,0:T(8,128)(2,1)S(1)} all-to-all(bf16[8,32,128]{2,1,0:T(8,128)(2,1)S(1)} %get-tuple-element.26), channel_id=1, replica_groups=mesh['kvp'=64,'tp'=8] {'tp'}, dimensions={0} | all-to-all | bytes 131072 | tf_op jit(solution)/shard_map/all_to_all | solution.py:247
  110.5 0.8 activate.1
  (2 shorter events, 0.0 us)
Async XLA Ops:
  0.6 64.0 %copy-start.2 = (bf16[2048,256]{1,0:T(8,128)(2,1)S(1)}, bf16[2048,256]{1,0:T(8,128)(2,1)}, u32[]{:S(2)}) copy-start(bf16[2048,256]{1,0:T(8,128)(2,1)} %weight.1) | copy-start | bytes 3145732
  3.1 23.3 %all-to-all-start = ((bf16[64,2,640]{2,1,0:T(2,128)(2,1)}), bf16[64,2,640]{2,1,0:T(2,128)(2,1)S(1)}, u32[]{:S(2)}, u32[]{:S(2)}) async-start(bf16[64,2,640]{2,1,0:T(2,128)(2,1)} %pack_inputs.1), calls=%async_computation | async-start | bytes 327680 | tf_op jit(solution)/shard_map/all_to_all | solution.py:247
  14.8 1.0 copy-start.3
  15.7 0.7 copy-start.4
  16.4 0.7 copy-start.5
  17.1 0.7 copy-start.6
  26.5 72.9 %copy-start.1 = (bf16[64,32,416]{2,1,0:T(8,128)(2,1)S(1)}, bf16[64,32,416]{2,1,0:T(8,128)(2,1)}, u32[]{:S(2)}) copy-start(bf16[64,32,416]{2,1,0:T(8,128)(2,1)} %up_weight.1) | copy-start | bytes 5111812
  27.6 71.9 %copy-start = (bf16[64,32,416]{2,1,0:T(8,128)(2,1)S(1)}, bf16[64,32,416]{2,1,0:T(8,128)(2,1)}, u32[]{:S(2)}) copy-start(bf16[64,32,416]{2,1,0:T(8,128)(2,1)} %gate_weight.1) | copy-start | bytes 5111812

commit v3 on v2

--- a/solution.py
+++ b/solution.py
@@ -59,13 +59,13 @@
         )
     q = jnp.concatenate(lines, axis=0)
     kv = [blocks[u, ROWS + w] for w in range(2) for u in range(STEPS)]
-    g = blocks[0, ROWS + 2]
-    g = jnp.concatenate([g[:1], g[1:]] * 2, axis=1)
-    line = jnp.concatenate([q] + kv + [jnp.concatenate([g, g], axis=0)], axis=1)
+    line = jnp.concatenate([q] + kv + [jnp.zeros((2, 2 * BATCH), f32)], axis=1)
     out[...] = jnp.broadcast_to(line.astype(bf16)[None], out.shape)
 
 
-def prepare(context, owner, pages, residual, keys, values, row_of, ordered, packed):
+def prepare(
+    context, owner, pages, residual, gain, keys, values, row_of, ordered, packed, gain_row
+):
     me = lax.axis_index("kvp")
     count, page_len = pages.shape[0], pages.shape[2]
     cache = pages[...].astype(f32)
@@ -79,6 +79,10 @@
         row = row + (page >= end).astype(jnp.int32)
     row_of[...] = row
     packed[...] = pack(residual[...].astype(f32))
+    line = gain[...].astype(f32)
+    gain_row[...] = jnp.broadcast_to(
+        jnp.concatenate([line] * 4, axis=1), gain_row.shape
+    )
 
     def one(c, carry):
         ordered[owner[me * count + c]] = pages[c].reshape(2 * page_len, HD)
@@ -87,7 +91,7 @@
     lax.fori_loop(0, count, one, 0, unroll=8)
 
 
-def attention(gathered, key_ref, value_ref, row_ref, out, gain_out):
+def attention(gathered, key_ref, value_ref, row_ref, gain_row, out):
     turned = gathered[...].astype(f32).T
     q = turned[: HEADS // KVH * BATCH].astype(bf16)
     fresh = turned[HEADS // KVH * BATCH :].astype(bf16)
@@ -95,19 +99,6 @@
     keys, values = key_ref[...], value_ref[...]
     combos, tokens = q.shape[0], keys.shape[0]
     peers = out.shape[0]
-    tail = gathered[...][:, combos + 2 * BATCH :]
-    take = lax.broadcasted_iota(jnp.int32, (peers, 2 * peers), 1) - 2 * lax.broadcasted_iota(
-        jnp.int32, (peers, 2 * peers), 0
-    )
-    gain_out[...] = jnp.concatenate(
-        [
-            jnp.dot(
-                jnp.where(take == k, 1.0, 0.0).astype(bf16), tail, preferred_element_type=f32
-            )
-            for k in range(2)
-        ],
-        axis=1,
-    )
     me = lax.axis_index("kvp")
     scale = HD ** (-0.5)
     nt = (((1,), (1,)), ((), ()))
@@ -140,15 +131,17 @@
     high = total.astype(bf16).astype(f32)
     lane = lax.broadcasted_iota(jnp.int32, (combos, HD), 1)
     stats = jnp.where(lane < 32, peak, jnp.where(lane < 64, high, total - high))
+    stats = jnp.where(lane < 96, stats, gain_row[...][:1])
     out[...] = jnp.concatenate(
         [numerator.reshape(peers, -1, HD), stats.reshape(peers, -1, HD)], axis=1
     ).astype(bf16)
 
 
-def merge(parts, ordered, out):
+def merge(parts, ordered, out, gain_out):
     x = parts[...].astype(f32)
     count = x.shape[1] // 2
     numerator, stats = x[:, :count], x[:, count:]
+    gain_out[...] = jnp.concatenate([stats[:, :1, 96:]] * 4, axis=2)
     peak = stats[:, :, 0:1]
     total = stats[:, :, 32:33] + stats[:, :, 64:65]
     top = jnp.max(peak, axis=0, keepdims=True)
@@ -163,18 +156,24 @@
     return jnp.concatenate([x[8 * q : 8 * q + 8] for q in range(4)], axis=1)
 
 
-def project(attended, weight, out):
+def project(attended, weight, residual, out):
     x = attended[...][:, 16:].astype(f32).reshape(-1, BATCH, HD).astype(bf16)
     flat = jnp.concatenate([x[h] for h in range(x.shape[0])], axis=1)
     acc = jnp.dot(flat, weight[...], preferred_element_type=f32)
-    for j in range(out.shape[0]):
-        out[j] = pack(acc[:, 32 * j : 32 * j + 32]).astype(bf16)
-
-
-def add_residual(parts, residual, own, sent):
-    total = jnp.sum(parts[...].astype(f32), axis=0)
-    value = (total + residual[...]).astype(bf16)
-    own[...] = value.astype(f32)
+    tp = out.shape[0] // 2
+    me = lax.axis_index("tp")
+    blocks = [
+        pack(acc[:, 32 * j : 32 * j + 32]) + jnp.where(me == j, residual[...], 0.0)
+        for j in range(tp)
+    ]
+    out[...] = jnp.stack(blocks * 2, axis=0).astype(bf16)
+
+
+def add_up(parts, own, sent):
+    total = jnp.sum(parts[...].astype(f32).reshape(2, -1, 8, HD), axis=1)
+    value = total.reshape(16, HD).astype(bf16)
+    wide = value.astype(f32)
+    own[...] = jnp.where(lax.axis_index("kvp") % 2 == 0, wide[:8], wide[8:])
     sent[...] = jnp.broadcast_to(value[None], sent.shape)
 
 
@@ -191,13 +190,13 @@
     ]
     for copy in copies:
         copy.start()
-    x = columns[...].astype(f32)
+    x = columns[...].astype(f32).reshape(-1, 8, HD)
     square = jnp.sum(x * x, axis=0)
     square = jnp.concatenate(
         [jnp.sum(square[:, 32 * q : 32 * q + 32], axis=1, keepdims=True) for q in range(4)],
         axis=0,
     )
-    scaled = (x * gain[...][:, None, :]).reshape(-1, 4, 8, HD)
+    scaled = (x * gain[...]).reshape(-1, 4, 8, HD)
     lane = lax.broadcasted_iota(jnp.int32, (scaled.shape[0], 8, HD), 2) // 32
     blocks = []
     for q in range(4):
@@ -243,8 +242,10 @@
     out[...] = (gated / (1.0 + jnp.exp(-gated)) * lifted).astype(bf16)
 
 
-def exchange(x, axis):
-    return lax.all_to_all(x, axis, split_axis=0, concat_axis=0, tiled=True)
+def exchange(x, axis, groups=None):
+    return lax.all_to_all(
+        x, axis, split_axis=0, concat_axis=0, tiled=True, axis_index_groups=groups
+    )
 
 
 def shards(
@@ -270,7 +271,6 @@
         [
             queries.transpose(0, 1, 3, 2),
             fresh_kv[:, :, :, 0].transpose(0, 2, 3, 1),
-            jnp.broadcast_to(norm_gain.reshape(1, 1, 2, ROWS), (STEPS, 1, 2, ROWS)),
         ],
         axis=1,
     )
@@ -282,7 +282,7 @@
         raw,
     )
     gathered = exchange(sent, "kvp")
-    keys, values, row_of, ordered, packed = call(
+    keys, values, row_of, ordered, packed, gain_row = call(
         prepare,
         "prepare",
         [
@@ -291,46 +291,60 @@
             shape((8, tokens), jnp.int32),
             shape((count, 2 * page_len, HD), bf16),
             shape((8, HD), f32),
+            shape((8, HD), f32),
         ],
-        [SMEM, SMEM, VMEM, VMEM],
+        [SMEM, SMEM, VMEM, VMEM, VMEM],
         context_pages,
         page_owner,
         kv_cache,
         residual,
-    )
-    parts, gain_rows = call(
+        norm_gain.reshape(1, -1),
+    )
+    parts = call(
         attention,
         "attention",
-        [shape((kvp, 2 * combos // kvp, HD), bf16), shape((kvp, HD), f32)],
-        [VMEM] * 4,
+        shape((kvp, 2 * combos // kvp, HD), bf16),
+        [VMEM] * 5,
         gathered.reshape(2 * kvp, -1),
         keys,
         values,
         row_of,
+        gain_row,
     )
     parts = exchange(parts, "kvp")
-    piece = call(
+    piece, gain_rows = call(
         merge,
         "merge",
-        shape((kvp, 2 * page_len + combos // kvp, HD), bf16),
+        [
+            shape((kvp, 2 * page_len + combos // kvp, HD), bf16),
+            shape((kvp, 1, HD), f32),
+        ],
         [VMEM] * 2,
         parts,
         ordered,
     )
     attended = exchange(piece, "kvp")
     partial = call(
-        project, "project", shape((tp, 8, HD), bf16), [VMEM, VMEM], attended, out_proj
-    )
-    summands = exchange(partial, "tp")
+        project,
+        "project",
+        shape((2 * tp, 8, HD), bf16),
+        [VMEM] * 3,
+        attended,
+        out_proj,
+        packed,
+    )
+    chips = kvp // 2
+    chip_line = [[chip * 2 * tp + k for k in range(2 * tp)] for chip in range(chips)]
+    same_core = [[2 * chip + core for chip in range(chips)] for core in range(2)]
+    summands = exchange(partial, ("kvp", "tp"), chip_line)
     own, block = call(
-        add_residual,
-        "add_residual",
-        [shape((8, HD), f32), shape((kvp, 8, HD), bf16)],
-        [VMEM, VMEM],
+        add_up,
+        "add_up",
+        [shape((8, HD), f32), shape((chips, 16, HD), bf16)],
+        [VMEM],
         summands,
-        packed,
-    )
-    columns = exchange(block, "kvp")
+    )
+    columns = exchange(block, "kvp", same_core)
     lifted, stream, regrouped = call(
         feed_forward,
         "feed_forward",

time: 112 us -> 110 us (0.982)
  the two profiles are of different devices: /device:TPU:1 before, /device:TPU:8 now
where the time goes in v3:
time: 110 us; the launch traced here: 109 us
  blocking collectives  80.8 us (73%)
  starting transfers between devices  10.6 us (10%)
  waiting for transfers between devices  6.19 us (6%)
  Pallas kernels  6 us (5%)
  local copies, waits for them, and re-layouts  3.75 us (3%)
    all_to_all x5, blocking collectives, exchange(): lax.all_to_all(x, axis, split_axis=0, concat_axis=0, tiled=True, axis_ind...  80.8 us
    all_to_all x1, starting transfers between devices, exchange(): lax.all_to_all(x, axis, split_axis=0, concat_axis=0, tiled=True, axis_ind...  10.6 us
    all_to_all x1, waiting for transfers between devices, exchange(): lax.all_to_all(x, axis, split_axis=0, concat_axis=0, tiled=True, axis_ind...  6.19 us
    pallas_call x8, Pallas kernels, call(): pl.pallas_call(body, out_shape=out_shape, in_specs=in_specs, out_specs=ou...  6 us
    unnamed x16, local copies, waits for them, and re-layouts  3.68 us
  transfers between devices with their start and end apart: 1, of which 1 were waited for; matrix products, arithmetic and copies ran while one was open for 0% of the time, Pallas kernels for 1%

profile of v3, /device:TPU:8, one launch (start us, length us, event | category | flops | bytes accessed | tf_op | source)
XLA Modules:
  0.0 108.9 jit_solution(16985159413979647504)
XLA Ops:
  0.6 0.0 copy-start.2
  0.6 0.9 pad_maximum_fusion.raw
  1.5 0.9 pack_inputs.1
  2.4 10.6 %all-to-all-start = ((bf16[64,2,640]{2,1,0:T(2,128)(2,1)}), bf16[64,2,640]{2,1,0:T(2,128)(2,1)S(1)}, u32[]{:S(2)}, u32[]{:S(2)}) async-start(bf16[64,2,640]{2,1,0:T(2,128)(2,1)} %pack_inputs.1), calls=%async_computation | async-start | bytes 327680 | tf_op jit(solution)/shard_map/all_to_all | solution.py:246
  13.0 0.0 copy-start.3
  13.0 0.9 copy-done.3
  13.9 0.0 copy-start.4
  13.9 0.7 copy-done.4
  14.6 0.0 copy-start.5
  14.6 0.7 copy-done.5
  15.3 0.0 copy-start.6
  15.3 0.7 copy-done.6
  16.0 0.0 copy-start.7
  16.0 0.7 copy-done.7
  16.6 1.0 prepare.1
  17.7 6.2 %all-to-all-done = bf16[64,2,640]{2,1,0:T(2,128)(2,1)S(1)} async-done(((bf16[64,2,640]{2,1,0:T(2,128)(2,1)}), bf16[64,2,640]{2,1,0:T(2,128)(2,1)S(1)}, u32[]{:S(2)}, u32[]{:S(2)}) %all-to-all-start) | async-done | bytes 163872 | tf_op jit(solution)/shard_map/all_to_all | solution.py:246
  23.8 0.1 reshape.15.gathered
  23.9 0.0 copy-start
  23.9 0.0 copy-start.1
  23.9 1.0 attention.1
  24.9 17.0 %all_to_all.30.parts = bf16[64,16,128]{2,1,0:T(8,128)(2,1)S(1)} all-to-all(bf16[64,16,128]{2,1,0:T(8,128)(2,1)S(1)} %attention.1), channel_id=1, replica_groups=mesh['kvp'=64,'tp'=8] {'kvp'}, dimensions={0} | all-to-all | bytes 524288 | tf_op jit(solution)/shard_map/all_to_all | solution.py:246
  41.9 0.4 merge.1
  42.3 19.6 %all_to_all.31.attended.pages = bf16[64,24,128]{2,1,0:T(8,128)(2,1)S(1)} all-to-all(bf16[64,24,128]{2,1,0:T(8,128)(2,1)S(1)} %get-tuple-element.21), channel_id=1, replica_groups=mesh['kvp'=64,'tp'=8] {'kvp'}, dimensions={0} | all-to-all | bytes 786432 | tf_op jit(solution)/shard_map/all_to_all | solution.py:246
  61.9 0.0 copy-done.2
  61.9 0.4 project.1
  62.3 18.1 %all_to_all.32.parts = bf16[16,8,128]{2,1,0:T(8,128)(2,1)S(1)} all-to-all(bf16[16,8,128]{2,1,0:T(8,128)(2,1)S(1)} %project.1), channel_id=1, replica_groups={{0,1,2,3,4,5,6,7,8,9,10,11,12,13,14,15},{16,17,18,19,20,21,22,23,24,25,..., dimensions={0} | all-to-all | bytes 65536 | tf_op jit(solution)/shard_map/all_to_all | solution.py:246
  80.4 15.4 %all_to_all.33.columns = bf16[32,16,128]{2,1,0:T(8,128)(2,1)S(1)} all-to-all(bf16[32,16,128]{2,1,0:T(8,128)(2,1)S(1)} %get-tuple-element.23), channel_id=1, replica_groups={{0,16,32,48,64,80,96,112,128,144,160,176,192,208,224,240,256,272,288,30..., dimensions={0} | all-to-all | bytes 262144 | tf_op jit(solution)/shard_map/all_to_all | solution.py:246
  95.8 0.0 copy-done
  95.8 0.0 copy-done.1
  95.8 1.6 %feed_forward.1 = (bf16[8,32,128]{2,1,0:T(8,128)(2,1)S(1)}, bf16[32,32]{1,0:T(8,128)(2,1)}, bf16[64,16,128]{2,1,0:T(8,128)(2,1)}) custom-call(bf16[32,16,128]{2,1,0:T(8,128)(2,1)S(1)} %all_to_all.33.columns, f32[64,1,128]{2,1,0:T(1,128)S(1)} %get-tuple-element.24.gain, bf16[64,32,416]{2,1,0:T(8,128)(2,1)S(1)} %copy-done, bf16[64,32,416]{2,1,0:T(8,128)(2,1)S(1)} %copy-done.1, ...), custom_call_target="tpu_custom_call" | custom-call | tf_op jit(solution)/shard_map/feed_forward/pallas_call | solution.py:29
  97.4 10.8 %all_to_all.34.parts = bf16[8,32,128]{2,1,0:T(8,128)(2,1)S(1)} all-to-all(bf16[8,32,128]{2,1,0:T(8,128)(2,1)S(1)} %get-tuple-element.28), channel_id=1, replica_groups=mesh['kvp'=64,'tp'=8] {'tp'}, dimensions={0} | all-to-all | bytes 131072 | tf_op jit(solution)/shard_map/all_to_all | solution.py:246
  108.1 0.8 activate.1
  (1 shorter events, 0.0 us)
Async XLA Ops:
  0.6 61.3 %copy-start.2 = (bf16[2048,256]{1,0:T(8,128)(2,1)S(1)}, bf16[2048,256]{1,0:T(8,128)(2,1)}, u32[]{:S(2)}) copy-start(bf16[2048,256]{1,0:T(8,128)(2,1)} %weight.1) | copy-start | bytes 3145732
  2.4 21.5 %all-to-all-start = ((bf16[64,2,640]{2,1,0:T(2,128)(2,1)}), bf16[64,2,640]{2,1,0:T(2,128)(2,1)S(1)}, u32[]{:S(2)}, u32[]{:S(2)}) async-start(bf16[64,2,640]{2,1,0:T(2,128)(2,1)} %pack_inputs.1), calls=%async_computation | async-start | bytes 327680 | tf_op jit(solution)/shard_map/all_to_all | solution.py:246
  13.0 1.0 copy-start.3
  13.9 0.7 copy-start.4
  14.6 0.7 copy-start.5
  15.3 0.7 copy-start.6
  16.0 0.7 copy-start.7
  23.9 71.9 %copy-start = (bf16[64,32,416]{2,1,0:T(8,128)(2,1)S(1)}, bf16[64,32,416]{2,1,0:T(8,128)(2,1)}, u32[]{:S(2)}) copy-start(bf16[64,32,416]{2,1,0:T(8,128)(2,1)} %gate_weight.1) | copy-start | bytes 5111812
  23.9 71.9 %copy-start.1 = (bf16[64,32,416]{2,1,0:T(8,128)(2,1)S(1)}, bf16[64,32,416]{2,1,0:T(8,128)(2,1)}, u32[]{:S(2)}) copy-start(bf16[64,32,416]{2,1,0:T(8,128)(2,1)} %up_weight.1) | copy-start | bytes 5111812

commit v4 on v3

--- a/solution.py
+++ b/solution.py
@@ -64,20 +64,21 @@
 
 
 def prepare(
-    context, owner, pages, residual, gain, keys, values, row_of, ordered, packed, gain_row
+    context, owner, pages, residual, gain, keys, values, member, ordered, packed, gain_row
 ):
     me = lax.axis_index("kvp")
     count, page_len = pages.shape[0], pages.shape[2]
     cache = pages[...].astype(f32)
     keys[...] = cache[:, 0].reshape(-1, HD).astype(bf16)
     values[...] = cache[:, 1].reshape(-1, HD).astype(bf16)
-    page = lax.broadcasted_iota(jnp.int32, row_of.shape, 1) // page_len + me * count
-    row = jnp.zeros(row_of.shape, jnp.int32)
+    page = lax.broadcasted_iota(jnp.int32, (8, member.shape[1]), 1) // page_len + me * count
+    row = jnp.zeros(page.shape, jnp.int32)
     end = jnp.int32(0)
     for r in range(ROWS - 1):
         end = end + context[r]
         row = row + (page >= end).astype(jnp.int32)
-    row_of[...] = row
+    line = lax.broadcasted_iota(jnp.int32, member.shape, 0) % ROWS
+    member[...] = jnp.where(row[:1] == line, 1.0, 0.0)
     packed[...] = pack(residual[...].astype(f32))
     line = gain[...].astype(f32)
     gain_row[...] = jnp.broadcast_to(
@@ -91,8 +92,8 @@
     lax.fori_loop(0, count, one, 0, unroll=8)
 
 
-def attention(gathered, key_ref, value_ref, row_ref, gain_row, out):
-    turned = gathered[...].astype(f32).T
+def attention(gathered, key_ref, value_ref, member_ref, gain_row, out):
+    turned = gathered[...].astype(f32).reshape(HD, -1).T
     q = turned[: HEADS // KVH * BATCH].astype(bf16)
     fresh = turned[HEADS // KVH * BATCH :].astype(bf16)
     fresh_k, fresh_v = fresh[:BATCH], fresh[BATCH : 2 * BATCH]
@@ -105,11 +106,12 @@
     scores = lax.dot_general(q, keys, nt, preferred_element_type=f32) * scale
     fresh_scores = lax.dot_general(q, fresh_k, nt, preferred_element_type=f32) * scale
 
-    row = row_ref[...][:1]
     combo = lax.broadcasted_iota(jnp.int32, (combos, 1), 0)
     combo_row = combo % ROWS
     combo_step = (combo // ROWS) % STEPS
-    member = combo_row == row
+    lines = member_ref.shape[0]
+    member = jnp.broadcast_to(member_ref[...][None], (combos // lines, lines, tokens))
+    member = member.reshape(combos, tokens) > 0.5
     entry = lax.broadcasted_iota(jnp.int32, (1, BATCH), 1)
     fresh_member = (
         (combo_row == entry % ROWS) & (entry // ROWS <= combo_step) & (me == 0)
@@ -129,26 +131,31 @@
         weights.astype(bf16), values, preferred_element_type=f32
     ) + jnp.dot(fresh_weights.astype(bf16), fresh_v, preferred_element_type=f32)
     high = total.astype(bf16).astype(f32)
-    lane = lax.broadcasted_iota(jnp.int32, (combos, HD), 1)
-    stats = jnp.where(lane < 32, peak, jnp.where(lane < 64, high, total - high))
-    stats = jnp.where(lane < 96, stats, gain_row[...][:1])
-    out[...] = jnp.concatenate(
-        [numerator.reshape(peers, -1, HD), stats.reshape(peers, -1, HD)], axis=1
-    ).astype(bf16)
+    columns = [x.reshape(peers, 8, 1) for x in (peak, high, total - high)]
+    lane = lax.broadcasted_iota(jnp.int32, (peers, 4, HD), 2)
+    stats = jnp.broadcast_to(gain_row[...][None, :4], (peers, 4, HD))
+    for k in range(5, -1, -1):
+        column = columns[k % 3][:, :4] if k < 3 else columns[k % 3][:, 4:]
+        stats = jnp.where(lane < 16 * k + 16, column, stats)
+    numerator = numerator.reshape(peers, 8, HD)
+    out[:, 0] = numerator[:, :4].astype(bf16)
+    out[:, 1] = numerator[:, 4:].astype(bf16)
+    out[:, 2] = stats.astype(bf16)
 
 
 def merge(parts, ordered, out, gain_out):
-    x = parts[...].astype(f32)
-    count = x.shape[1] // 2
-    numerator, stats = x[:, :count], x[:, count:]
+    stats = parts[:, 2].astype(f32)
     gain_out[...] = jnp.concatenate([stats[:, :1, 96:]] * 4, axis=2)
-    peak = stats[:, :, 0:1]
-    total = stats[:, :, 32:33] + stats[:, :, 64:65]
-    top = jnp.max(peak, axis=0, keepdims=True)
-    factor = jnp.exp(peak - top)
-    denominator = jnp.sum(factor * total, axis=0)
-    value = jnp.sum(factor * numerator, axis=0) / denominator
-    value = jnp.broadcast_to(value.astype(bf16)[None], (out.shape[0],) + value.shape)
+    values = []
+    for half in range(2):
+        at = 48 * half
+        peak = stats[:, :, at : at + 1]
+        total = stats[:, :, at + 16 : at + 17] + stats[:, :, at + 32 : at + 33]
+        factor = jnp.exp(peak - jnp.max(peak, axis=0, keepdims=True))
+        numerator = jnp.sum(factor * parts[:, half].astype(f32), axis=0)
+        values.append(numerator / jnp.sum(factor * total, axis=0))
+    value = jnp.concatenate(values, axis=0).astype(bf16)
+    value = jnp.broadcast_to(value[None], (out.shape[0],) + value.shape)
     out[...] = jnp.concatenate([ordered[...], value], axis=1)
 
 
@@ -282,13 +289,13 @@
         raw,
     )
     gathered = exchange(sent, "kvp")
-    keys, values, row_of, ordered, packed, gain_row = call(
+    keys, values, member, ordered, packed, gain_row = call(
         prepare,
         "prepare",
         [
             shape((tokens, HD), bf16),
             shape((tokens, HD), bf16),
-            shape((8, tokens), jnp.int32),
+            shape((16 * ROWS, tokens), f32),
             shape((count, 2 * page_len, HD), bf16),
             shape((8, HD), f32),
             shape((8, HD), f32),
@@ -303,12 +310,12 @@
     parts = call(
         attention,
         "attention",
-        shape((kvp, 2 * combos // kvp, HD), bf16),
+        shape((kvp, 3, 4, HD), bf16),
         [VMEM] * 5,
-        gathered.reshape(2 * kvp, -1),
+        gathered,
         keys,
         values,
-        row_of,
+        member,
         gain_row,
     )
     parts = exchange(parts, "kvp")

time: 110 us -> 108 us (0.982)
  blocking collectives: 80.8 us -> 79.5 us
    all_to_all x5, blocking collectives: 80.8 us -> 79.5 us  [exchange(): lax.all_to_all(x, axis, split_axis=0, concat_axis=0, tiled=True, axis_ind...]
where the time goes in v4:
time: 108 us
  blocking collectives  79.5 us (74%)
  starting transfers between devices  10.6 us (10%)
  Pallas kernels  6.41 us (6%)
  waiting for transfers between devices  6.15 us (6%)
  local copies, waits for them, and re-layouts  3.68 us (3%)
    all_to_all x5, blocking collectives, exchange(): lax.all_to_all(x, axis, split_axis=0, concat_axis=0, tiled=True, axis_ind...  79.5 us
    all_to_all x1, starting transfers between devices, exchange(): lax.all_to_all(x, axis, split_axis=0, concat_axis=0, tiled=True, axis_ind...  10.6 us
    pallas_call x8, Pallas kernels, call(): pl.pallas_call(body, out_shape=out_shape, in_specs=in_specs, out_specs=ou...  6.41 us
    all_to_all x1, waiting for transfers between devices, exchange(): lax.all_to_all(x, axis, split_axis=0, concat_axis=0, tiled=True, axis_ind...  6.15 us
    unnamed x16, local copies, waits for them, and re-layouts  3.68 us
  transfers between devices with their start and end apart: 1, of which 1 were waited for; matrix products, arithmetic and copies ran while one was open for 0% of the time, Pallas kernels for 1%

profile of v4, /device:TPU:8, one launch (start us, length us, event | category | flops | bytes accessed | tf_op | source)
XLA Modules:
  0.0 107.8 jit_solution(1323191297074099894)
XLA Ops:
  0.6 0.0 copy-start.2
  0.6 0.9 pad_maximum_fusion.raw
  1.5 0.9 pack_inputs.1
  2.4 10.6 %all-to-all-start = ((bf16[64,2,640]{2,1,0:T(2,128)(2,1)}), bf16[64,2,640]{2,1,0:T(2,128)(2,1)S(1)}, u32[]{:S(2)}, u32[]{:S(2)}) async-start(bf16[64,2,640]{2,1,0:T(2,128)(2,1)} %pack_inputs.1), calls=%async_computation | async-start | bytes 327680 | tf_op jit(solution)/shard_map/all_to_all | solution.py:253
  13.0 0.0 copy-start.3
  13.0 0.9 copy-done.3
  13.9 0.0 copy-start.4
  13.9 0.7 copy-done.4
  14.6 0.0 copy-start.5
  14.6 0.7 copy-done.5
  15.3 0.0 copy-start.6
  15.3 0.7 copy-done.6
  16.0 0.0 copy-start.7
  16.0 0.7 copy-done.7
  16.6 1.0 prepare.1
  17.7 6.1 %all-to-all-done.gathered = bf16[64,2,640]{2,1,0:T(2,128)(2,1)S(1)} async-done(((bf16[64,2,640]{2,1,0:T(2,128)(2,1)}), bf16[64,2,640]{2,1,0:T(2,128)(2,1)S(1)}, u32[]{:S(2)}, u32[]{:S(2)}) %all-to-all-start) | async-done | bytes 163872 | tf_op jit(solution)/shard_map/all_to_all | solution.py:253
  23.8 0.0 copy-start
  23.8 0.0 copy-start.1
  23.8 1.1 %attention.1 = bf16[64,3,4,128]{3,2,1,0:T(4,128)(2,1)S(1)} custom-call(bf16[64,2,640]{2,1,0:T(2,128)(2,1)S(1)} %all-to-all-done.gathered, bf16[512,128]{1,0:T(8,128)(2,1)S(1)} %get-tuple-element.16.key_ref, bf16[512,128]{1,0:T(8,128)(2,1)S(1)} %get-tuple-element.17.value_ref, f32[256,512]{1,0:T(8,128)S(1)} %get-tuple-element.18.member_ref, ...), custom_call_target="tpu_custom_call" | custom-call | tf_op jit(solution)/shard_map/attention/pallas_call | solution.py:29
  24.9 16.2 %all_to_all.30.parts = bf16[64,3,4,128]{3,2,1,0:T(4,128)(2,1)S(1)} all-to-all(bf16[64,3,4,128]{3,2,1,0:T(4,128)(2,1)S(1)} %attention.1), channel_id=1, replica_groups=mesh['kvp'=64,'tp'=8] {'kvp'}, dimensions={0} | all-to-all | bytes 393216 | tf_op jit(solution)/shard_map/all_to_all | solution.py:253
  41.1 0.6 merge.1
  41.7 19.1 %all_to_all.31.attended.pages = bf16[64,24,128]{2,1,0:T(8,128)(2,1)S(1)} all-to-all(bf16[64,24,128]{2,1,0:T(8,128)(2,1)S(1)} %get-tuple-element.21), channel_id=1, replica_groups=mesh['kvp'=64,'tp'=8] {'kvp'}, dimensions={0} | all-to-all | bytes 786432 | tf_op jit(solution)/shard_map/all_to_all | solution.py:253
  60.8 0.0 copy-done.2
  60.8 0.4 project.1
  61.2 18.1 %all_to_all.32.parts = bf16[16,8,128]{2,1,0:T(8,128)(2,1)S(1)} all-to-all(bf16[16,8,128]{2,1,0:T(8,128)(2,1)S(1)} %project.1), channel_id=1, replica_groups={{0,1,2,3,4,5,6,7,8,9,10,11,12,13,14,15},{16,17,18,19,20,21,22,23,24,25,..., dimensions={0} | all-to-all | bytes 65536 | tf_op jit(solution)/shard_map/all_to_all | solution.py:253
  79.3 15.4 %all_to_all.33.columns = bf16[32,16,128]{2,1,0:T(8,128)(2,1)S(1)} all-to-all(bf16[32,16,128]{2,1,0:T(8,128)(2,1)S(1)} %get-tuple-element.23), channel_id=1, replica_groups={{0,16,32,48,64,80,96,112,128,144,160,176,192,208,224,240,256,272,288,30..., dimensions={0} | all-to-all | bytes 262144 | tf_op jit(solution)/shard_map/all_to_all | solution.py:253
  94.7 0.0 copy-done
  94.7 0.0 copy-done.1
  94.7 1.6 %feed_forward.1 = (bf16[8,32,128]{2,1,0:T(8,128)(2,1)S(1)}, bf16[32,32]{1,0:T(8,128)(2,1)}, bf16[64,16,128]{2,1,0:T(8,128)(2,1)}) custom-call(bf16[32,16,128]{2,1,0:T(8,128)(2,1)S(1)} %all_to_all.33.columns, f32[64,1,128]{2,1,0:T(1,128)S(1)} %get-tuple-element.24.gain, bf16[64,32,416]{2,1,0:T(8,128)(2,1)S(1)} %copy-done, bf16[64,32,416]{2,1,0:T(8,128)(2,1)S(1)} %copy-done.1, ...), custom_call_target="tpu_custom_call" | custom-call | tf_op jit(solution)/shard_map/feed_forward/pallas_call | solution.py:29
  96.3 10.8 %all_to_all.34.parts = bf16[8,32,128]{2,1,0:T(8,128)(2,1)S(1)} all-to-all(bf16[8,32,128]{2,1,0:T(8,128)(2,1)S(1)} %get-tuple-element.28), channel_id=1, replica_groups=mesh['kvp'=64,'tp'=8] {'tp'}, dimensions={0} | all-to-all | bytes 131072 | tf_op jit(solution)/shard_map/all_to_all | solution.py:253
  107.0 0.8 activate.1
  (1 shorter events, 0.0 us)
Async XLA Ops:
  0.6 60.2 %copy-start.2 = (bf16[2048,256]{1,0:T(8,128)(2,1)S(1)}, bf16[2048,256]{1,0:T(8,128)(2,1)}, u32[]{:S(2)}) copy-start(bf16[2048,256]{1,0:T(8,128)(2,1)} %weight.1) | copy-start | bytes 3145732
  2.4 21.5 %all-to-all-start = ((bf16[64,2,640]{2,1,0:T(2,128)(2,1)}), bf16[64,2,640]{2,1,0:T(2,128)(2,1)S(1)}, u32[]{:S(2)}, u32[]{:S(2)}) async-start(bf16[64,2,640]{2,1,0:T(2,128)(2,1)} %pack_inputs.1), calls=%async_computation | async-start | bytes 327680 | tf_op jit(solution)/shard_map/all_to_all | solution.py:253
  13.0 1.0 copy-start.3
  13.9 0.7 copy-start.4
  14.6 0.7 copy-start.5
  15.3 0.7 copy-start.6
  16.0 0.7 copy-start.7
  23.8 70.8 %copy-start = (bf16[64,32,416]{2,1,0:T(8,128)(2,1)S(1)}, bf16[64,32,416]{2,1,0:T(8,128)(2,1)}, u32[]{:S(2)}) copy-start(bf16[64,32,416]{2,1,0:T(8,128)(2,1)} %gate_weight.1) | copy-start | bytes 5111812
  23.8 70.8 %copy-start.1 = (bf16[64,32,416]{2,1,0:T(8,128)(2,1)S(1)}, bf16[64,32,416]{2,1,0:T(8,128)(2,1)}, u32[]{:S(2)}) copy-start(bf16[64,32,416]{2,1,0:T(8,128)(2,1)} %up_weight.1) | copy-start | bytes 5111812

commit v5 on v4

--- a/solution.py
+++ b/solution.py
@@ -12,6 +12,7 @@
 STEPS = 2
 ROWS = 16
 BATCH = STEPS * ROWS
+LINES = 4 * ROWS
 
 negative = -1e30
 epsilon = 1e-05
@@ -59,47 +60,66 @@
         )
     q = jnp.concatenate(lines, axis=0)
     kv = [blocks[u, ROWS + w] for w in range(2) for u in range(STEPS)]
-    line = jnp.concatenate([q] + kv + [jnp.zeros((2, 2 * BATCH), f32)], axis=1)
-    out[...] = jnp.broadcast_to(line.astype(bf16)[None], out.shape)
+    tail = kv + [blocks[0, ROWS + 2], blocks[0, ROWS + 3]] * 2
+    half = q.shape[1] // 2
+    lines = [
+        jnp.concatenate([q[:, c * half : c * half + half]] + tail, axis=1).astype(bf16)
+        for c in range(2)
+    ]
+    sent = jnp.stack(lines, axis=0)[None]
+    out[...] = jnp.broadcast_to(sent, (out.shape[0] // 2,) + sent.shape[1:]).reshape(out.shape)
 
 
 def prepare(
-    context, owner, pages, residual, gain, keys, values, member, ordered, packed, gain_row
+    numbers, pages, residual, keys, values, member, ordered, packed
 ):
     me = lax.axis_index("kvp")
-    count, page_len = pages.shape[0], pages.shape[2]
-    cache = pages[...].astype(f32)
-    keys[...] = cache[:, 0].reshape(-1, HD).astype(bf16)
-    values[...] = cache[:, 1].reshape(-1, HD).astype(bf16)
-    page = lax.broadcasted_iota(jnp.int32, (8, member.shape[1]), 1) // page_len + me * count
+    count, page_len = pages.shape[1], pages.shape[3]
+    half = count * page_len
+    for c in range(2):
+        cache = pages[c].astype(f32)
+        keys[c * half : c * half + half] = cache[:, 0].reshape(-1, HD).astype(bf16)
+        values[c * half : c * half + half] = cache[:, 1].reshape(-1, HD).astype(bf16)
+    page = lax.broadcasted_iota(jnp.int32, (8, member.shape[1]), 1) // page_len
+    page = page + me // 2 * 2 * count
     row = jnp.zeros(page.shape, jnp.int32)
     end = jnp.int32(0)
     for r in range(ROWS - 1):
-        end = end + context[r]
+        end = end + numbers[r]
         row = row + (page >= end).astype(jnp.int32)
     line = lax.broadcasted_iota(jnp.int32, member.shape, 0) % ROWS
     member[...] = jnp.where(row[:1] == line, 1.0, 0.0)
     packed[...] = pack(residual[...].astype(f32))
-    line = gain[...].astype(f32)
-    gain_row[...] = jnp.broadcast_to(
-        jnp.concatenate([line] * 4, axis=1), gain_row.shape
-    )
 
     def one(c, carry):
-        ordered[owner[me * count + c]] = pages[c].reshape(2 * page_len, HD)
+        ordered[numbers[ROWS + me * count + c]] = pages[me % 2, c].reshape(2 * page_len, HD)
         return carry
 
     lax.fori_loop(0, count, one, 0, unroll=8)
 
 
-def attention(gathered, key_ref, value_ref, member_ref, gain_row, out):
+def attention(gathered, key_ref, value_ref, member_ref, out, gain_out):
     turned = gathered[...].astype(f32).reshape(HD, -1).T
-    q = turned[: HEADS // KVH * BATCH].astype(bf16)
-    fresh = turned[HEADS // KVH * BATCH :].astype(bf16)
+    combos = HEADS // KVH // 2 * BATCH
+    q = turned[:combos].astype(bf16)
+    fresh = turned[combos:].astype(bf16)
     fresh_k, fresh_v = fresh[:BATCH], fresh[BATCH : 2 * BATCH]
     keys, values = key_ref[...], value_ref[...]
-    combos, tokens = q.shape[0], keys.shape[0]
+    tokens = keys.shape[0]
     peers = out.shape[0]
+    tail = gathered[...].astype(f32).reshape(HD, -1)[:, combos + 2 * BATCH :].astype(bf16)
+    take = lax.broadcasted_iota(jnp.int32, (HD // 2, HD), 1) - 2 * lax.broadcasted_iota(
+        jnp.int32, (HD // 2, HD), 0
+    )
+    gain_out[...] = jnp.concatenate(
+        [
+            jnp.dot(
+                jnp.where(take == k, 1.0, 0.0).astype(bf16), tail, preferred_element_type=f32
+            )
+            for k in range(2)
+        ],
+        axis=1,
+    )
     me = lax.axis_index("kvp")
     scale = HD ** (-0.5)
     nt = (((1,), (1,)), ((), ()))
@@ -114,7 +134,7 @@
     member = member.reshape(combos, tokens) > 0.5
     entry = lax.broadcasted_iota(jnp.int32, (1, BATCH), 1)
     fresh_member = (
-        (combo_row == entry % ROWS) & (entry // ROWS <= combo_step) & (me == 0)
+        (combo_row == entry % ROWS) & (entry // ROWS <= combo_step) & (me // 2 == 0)
     )
     scores = jnp.where(member, scores, negative)
     fresh_scores = jnp.where(fresh_member, fresh_scores, negative)
@@ -133,7 +153,7 @@
     high = total.astype(bf16).astype(f32)
     columns = [x.reshape(peers, 8, 1) for x in (peak, high, total - high)]
     lane = lax.broadcasted_iota(jnp.int32, (peers, 4, HD), 2)
-    stats = jnp.broadcast_to(gain_row[...][None, :4], (peers, 4, HD))
+    stats = jnp.zeros((peers, 4, HD), f32)
     for k in range(5, -1, -1):
         column = columns[k % 3][:, :4] if k < 3 else columns[k % 3][:, 4:]
         stats = jnp.where(lane < 16 * k + 16, column, stats)
@@ -143,9 +163,8 @@
     out[:, 2] = stats.astype(bf16)
 
 
-def merge(parts, ordered, out, gain_out):
+def merge(parts, ordered, out):
     stats = parts[:, 2].astype(f32)
-    gain_out[...] = jnp.concatenate([stats[:, :1, 96:]] * 4, axis=2)
     values = []
     for half in range(2):
         at = 48 * half
@@ -164,7 +183,9 @@
 
 
 def project(attended, weight, residual, out):
-    x = attended[...][:, 16:].astype(f32).reshape(-1, BATCH, HD).astype(bf16)
+    x = attended[...][:, 16:].astype(f32).reshape(-1, 2, 8, HD)
+    x = jnp.concatenate([x[:, c].reshape(-1, BATCH, HD) for c in range(2)], axis=0)
+    x = x.astype(bf16)
     flat = jnp.concatenate([x[h] for h in range(x.shape[0])], axis=1)
     acc = jnp.dot(flat, weight[...], preferred_element_type=f32)
     tp = out.shape[0] // 2
@@ -203,7 +224,7 @@
         [jnp.sum(square[:, 32 * q : 32 * q + 32], axis=1, keepdims=True) for q in range(4)],
         axis=0,
     )
-    scaled = (x * gain[...]).reshape(-1, 4, 8, HD)
+    scaled = (x * gain[...][:, None, :]).reshape(-1, 4, 8, HD)
     lane = lax.broadcasted_iota(jnp.int32, (scaled.shape[0], 8, HD), 2) // 32
     blocks = []
     for q in range(4):
@@ -273,59 +294,59 @@
     combos = queries.shape[2] * BATCH
 
     count, page_len = kv_cache.shape[0], kv_cache.shape[2]
-    tokens = count * page_len
+    tokens = 2 * count * page_len
     raw = jnp.concatenate(
         [
             queries.transpose(0, 1, 3, 2),
             fresh_kv[:, :, :, 0].transpose(0, 2, 3, 1),
+            lax.broadcast_in_dim(norm_gain[:ROWS], (STEPS, 1, 2, ROWS), (3,)),
+            lax.broadcast_in_dim(norm_gain[ROWS:], (STEPS, 1, 2, ROWS), (3,)),
         ],
         axis=1,
     )
     sent = call(
         pack_inputs,
         "pack_inputs",
-        shape((kvp, 2, combos + 4 * BATCH), bf16),
+        shape((kvp, 2, combos // 2 + 4 * BATCH), bf16),
         [VMEM],
         raw,
     )
     gathered = exchange(sent, "kvp")
-    keys, values, member, ordered, packed, gain_row = call(
+    chips = kvp // 2
+    chip_line = [[chip * 2 * tp + k for k in range(2 * tp)] for chip in range(chips)]
+    same_core = [[2 * chip + core for chip in range(chips)] for core in range(2)]
+    same_chip = [[2 * chip, 2 * chip + 1] for chip in range(chips)]
+    pages = lax.all_gather(kv_cache, "kvp", axis_index_groups=same_chip)
+    keys, values, member, ordered, packed = call(
         prepare,
         "prepare",
         [
             shape((tokens, HD), bf16),
             shape((tokens, HD), bf16),
-            shape((16 * ROWS, tokens), f32),
+            shape((LINES, tokens), f32),
             shape((count, 2 * page_len, HD), bf16),
             shape((8, HD), f32),
-            shape((8, HD), f32),
         ],
-        [SMEM, SMEM, VMEM, VMEM, VMEM],
-        context_pages,
-        page_owner,
-        kv_cache,
+        [SMEM, VMEM, VMEM],
+        jnp.concatenate([context_pages, page_owner]),
+        pages,
         residual,
-        norm_gain.reshape(1, -1),
-    )
-    parts = call(
+    )
+    parts, gain_rows = call(
         attention,
         "attention",
-        shape((kvp, 3, 4, HD), bf16),
-        [VMEM] * 5,
+        [shape((chips, 3, 4, HD), bf16), shape((kvp, HD), f32)],
+        [VMEM] * 4,
         gathered,
         keys,
         values,
         member,
-        gain_row,
-    )
-    parts = exchange(parts, "kvp")
-    piece, gain_rows = call(
+    )
+    parts = exchange(parts, "kvp", same_core)
+    piece = call(
         merge,
         "merge",
-        [
-            shape((kvp, 2 * page_len + combos // kvp, HD), bf16),
-            shape((kvp, 1, HD), f32),
-        ],
+        shape((kvp, 2 * page_len + 8, HD), bf16),
         [VMEM] * 2,
         parts,
         ordered,
@@ -340,9 +361,6 @@
         out_proj,
         packed,
     )
-    chips = kvp // 2
-    chip_line = [[chip * 2 * tp + k for k in range(2 * tp)] for chip in range(chips)]
-    same_core = [[2 * chip + core for chip in range(chips)] for core in range(2)]
     summands = exchange(partial, ("kvp", "tp"), chip_line)
     own, block = call(
         add_up,

time: 108 us -> 106 us (0.981)
  local copies, waits for them, and re-layouts: 3.68 us -> 1.52 us
  waiting for transfers between devices: 6.15 us -> 4.54 us
    unnamed x16 -> x8, local copies, waits for them, and re-layouts: 3.68 us -> 0.71 us
    all_gather x0 -> x1, blocking collectives: none -> 2.38 us  [shards(): pages = lax.all_gather(kv_cache, 'kvp', axis_index_groups=same_chip)]
    all_to_all x5, blocking collectives: 79.5 us -> 77.5 us  [exchange(): lax.all_to_all(x, axis, split_axis=0, concat_axis=0, tiled=True, axis_ind...]
    all_to_all x1, waiting for transfers between devices: 6.15 us -> 4.54 us  [exchange(): lax.all_to_all(x, axis, split_axis=0, concat_axis=0, tiled=True, axis_ind...]
  transfers between devices with their start and end apart: 1 -> 1, of which waited for: 1 -> 1; matrix products, arithmetic and copies ran while one was open for 0% -> 1% of each run, Pallas kernels for 1% -> 1%
where the time goes in v5:
time: 106 us; the launch traced here: 105 us
  blocking collectives  79.9 us (75%)
  starting transfers between devices  10.7 us (10%)
  Pallas kernels  6.09 us (6%)
  waiting for transfers between devices  4.54 us (4%)
  other arithmetic  1.57 us (1%)
  local copies, waits for them, and re-layouts  1.52 us (1%)
    all_to_all x5, blocking collectives, exchange(): lax.all_to_all(x, axis, split_axis=0, concat_axis=0, tiled=True, axis_ind...  77.5 us
    all_to_all x1, starting transfers between devices, exchange(): lax.all_to_all(x, axis, split_axis=0, concat_axis=0, tiled=True, axis_ind...  10.7 us
    pallas_call x8, Pallas kernels, call(): pl.pallas_call(body, out_shape=out_shape, in_specs=in_specs, out_specs=ou...  6.09 us
    all_to_all x1, waiting for transfers between devices, exchange(): lax.all_to_all(x, axis, split_axis=0, concat_axis=0, tiled=True, axis_ind...  4.54 us
    all_gather x1, blocking collectives, shards(): pages = lax.all_gather(kv_cache, 'kvp', axis_index_groups=same_chip)  2.38 us
  transfers between devices with their start and end apart: 1, of which 1 were waited for; matrix products, arithmetic and copies ran while one was open for 1% of the time, Pallas kernels for 1%

profile of v5, /device:TPU:8, one launch (start us, length us, event | category | flops | bytes accessed | tf_op | source)
XLA Modules:
  0.0 105.0 jit_solution(17551443692808112349)
XLA Ops:
  0.6 0.8 fusion
  1.4 0.8 pad_maximum_fusion.raw
  2.2 0.9 pack_inputs.1
  3.1 0.0 copy-start.2
  3.1 10.7 %all-to-all-start = ((bf16[64,2,384]{2,1,0:T(2,128)(2,1)}), bf16[64,2,384]{2,1,0:T(2,128)(2,1)S(1)}, u32[]{:S(2)}, u32[]{:S(2)}) async-start(bf16[64,2,384]{2,1,0:T(2,128)(2,1)} %pack_inputs.1), calls=%async_computation | async-start | bytes 196608 | tf_op jit(solution)/shard_map/all_to_all | solution.py:274
  13.8 0.8 pad_add_fusion.numbers
  14.6 2.4 %all-gather = bf16[128,2,8,128]{3,2,1,0:T(8,128)(2,1)S(1)} all-gather(bf16[64,2,8,128]{3,2,1,0:T(8,128)(2,1)} %param.12), channel_id=2, replica_groups={{0,8},{16,24},{32,40},{48,56},{64,72},{80,88},{96,104},{112,120},{128,1..., dimensions={0}, use_global_device_ids=true | all-gather | bytes 786432 | tf_op jit(solution)/shard_map/all_gather | solution.py:319
  17.0 0.0 copy-start.3
  17.0 0.7 copy-done.3
  17.7 1.1 %prepare.1 = (bf16[1024,128]{1,0:T(8,128)(2,1)S(1)}, bf16[1024,128]{1,0:T(8,128)(2,1)S(1)}, f32[64,1024]{1,0:T(8,128)S(1)}, bf16[64,16,128]{2,1,0:T(8,128)(2,1)S(1)}, f32[8,128]{1,0:T(8,128)S(1)}) custom-call(s32[4112]{0:T(1024)S(1)} %pad_add_fusion.numbers, bf16[2,64,2,8,128]{4,3,2,1,0:T(8,128)(2,1)S(1)} %bitcast.6, bf16[32,32]{1,0:T(8,128)(2,1)S(1)} %copy-done.3), custom_call_target="tpu_custom_call" | custom-call | tf_op jit(solution)/shard_map/prepare/pallas_call | solution.py:30
  18.8 4.5 %all-to-all-done.gathered = bf16[64,2,384]{2,1,0:T(2,128)(2,1)S(1)} async-done(((bf16[64,2,384]{2,1,0:T(2,128)(2,1)}), bf16[64,2,384]{2,1,0:T(2,128)(2,1)S(1)}, u32[]{:S(2)}, u32[]{:S(2)}) %all-to-all-start) | async-done | bytes 98336 | tf_op jit(solution)/shard_map/all_to_all | solution.py:274
  23.3 0.0 copy-start
  23.3 0.0 copy-start.1
  23.3 1.0 attention.1
  24.4 14.7 %all_to_all.30.parts = bf16[32,3,4,128]{3,2,1,0:T(4,128)(2,1)S(1)} all-to-all(bf16[32,3,4,128]{3,2,1,0:T(4,128)(2,1)S(1)} %get-tuple-element.18), channel_id=1, replica_groups={{0,16,32,48,64,80,96,112,128,144,160,176,192,208,224,240,256,272,288,30..., dimensions={0} | all-to-all | bytes 196608 | tf_op jit(solution)/shard_map/all_to_all | solution.py:274
  39.1 0.3 merge.1
  39.4 18.6 %all_to_all.31.attended.pages = bf16[64,24,128]{2,1,0:T(8,128)(2,1)S(1)} all-to-all(bf16[64,24,128]{2,1,0:T(8,128)(2,1)S(1)} %merge.1), channel_id=1, replica_groups=mesh['kvp'=64,'tp'=8] {'kvp'}, dimensions={0} | all-to-all | bytes 786432 | tf_op jit(solution)/shard_map/all_to_all | solution.py:274
  57.9 0.0 copy-done.2
  57.9 0.4 project.1
  58.3 18.1 %all_to_all.32.parts = bf16[16,8,128]{2,1,0:T(8,128)(2,1)S(1)} all-to-all(bf16[16,8,128]{2,1,0:T(8,128)(2,1)S(1)} %project.1), channel_id=1, replica_groups={{0,1,2,3,4,5,6,7,8,9,10,11,12,13,14,15},{16,17,18,19,20,21,22,23,24,25,..., dimensions={0} | all-to-all | bytes 65536 | tf_op jit(solution)/shard_map/all_to_all | solution.py:274
  76.5 15.3 %all_to_all.33.columns = bf16[32,16,128]{2,1,0:T(8,128)(2,1)S(1)} all-to-all(bf16[32,16,128]{2,1,0:T(8,128)(2,1)S(1)} %get-tuple-element.21), channel_id=1, replica_groups={{0,16,32,48,64,80,96,112,128,144,160,176,192,208,224,240,256,272,288,30..., dimensions={0} | all-to-all | bytes 262144 | tf_op jit(solution)/shard_map/all_to_all | solution.py:274
  91.8 0.0 copy-done
  91.8 0.0 copy-done.1
  91.8 1.6 %feed_forward.1 = (bf16[8,32,128]{2,1,0:T(8,128)(2,1)S(1)}, bf16[32,32]{1,0:T(8,128)(2,1)}, bf16[64,16,128]{2,1,0:T(8,128)(2,1)}) custom-call(bf16[32,16,128]{2,1,0:T(8,128)(2,1)S(1)} %all_to_all.33.columns, f32[64,128]{1,0:T(8,128)S(1)} %get-tuple-element.22.gain, bf16[64,32,416]{2,1,0:T(8,128)(2,1)S(1)} %copy-done, bf16[64,32,416]{2,1,0:T(8,128)(2,1)S(1)} %copy-done.1, ...), custom_call_target="tpu_custom_call" | custom-call | tf_op jit(solution)/shard_map/feed_forward/pallas_call | solution.py:30
  93.4 10.8 %all_to_all.34.parts = bf16[8,32,128]{2,1,0:T(8,128)(2,1)S(1)} all-to-all(bf16[8,32,128]{2,1,0:T(8,128)(2,1)S(1)} %get-tuple-element.26), channel_id=1, replica_groups=mesh['kvp'=64,'tp'=8] {'tp'}, dimensions={0} | all-to-all | bytes 131072 | tf_op jit(solution)/shard_map/all_to_all | solution.py:274
  104.1 0.8 activate.1
  (3 shorter events, 0.0 us)
Async XLA Ops:
  3.1 54.8 %copy-start.2 = (bf16[2048,256]{1,0:T(8,128)(2,1)S(1)}, bf16[2048,256]{1,0:T(8,128)(2,1)}, u32[]{:S(2)}) copy-start(bf16[2048,256]{1,0:T(8,128)(2,1)} %weight.1) | copy-start | bytes 3145732
  3.1 20.2 %all-to-all-start = ((bf16[64,2,384]{2,1,0:T(2,128)(2,1)}), bf16[64,2,384]{2,1,0:T(2,128)(2,1)S(1)}, u32[]{:S(2)}, u32[]{:S(2)}) async-start(bf16[64,2,384]{2,1,0:T(2,128)(2,1)} %pack_inputs.1), calls=%async_computation | async-start | bytes 196608 | tf_op jit(solution)/shard_map/all_to_all | solution.py:274
  17.0 0.7 copy-start.3
  23.3 68.5 %copy-start = (bf16[64,32,416]{2,1,0:T(8,128)(2,1)S(1)}, bf16[64,32,416]{2,1,0:T(8,128)(2,1)}, u32[]{:S(2)}) copy-start(bf16[64,32,416]{2,1,0:T(8,128)(2,1)} %gate_weight.1) | copy-start | bytes 5111812
  23.3 68.5 %copy-start.1 = (bf16[64,32,416]{2,1,0:T(8,128)(2,1)S(1)}, bf16[64,32,416]{2,1,0:T(8,128)(2,1)}, u32[]{:S(2)}) copy-start(bf16[64,32,416]{2,1,0:T(8,128)(2,1)} %up_weight.1) | copy-start | bytes 5111812

commit v6 on v5

--- a/solution.py
+++ b/solution.py
@@ -20,11 +20,12 @@
 f32 = jnp.float32
 VMEM = pl.BlockSpec(memory_space=pltpu.VMEM)
 SMEM = pl.BlockSpec(memory_space=pltpu.SMEM)
-PARAMS = pltpu.CompilerParams(vmem_limit_bytes=16 * 1024 * 1024)
+MIB = 1024 * 1024
+ALL = 60 * MIB
 HBM = pl.BlockSpec(memory_space=pltpu.HBM)
 
 
-def call(body, name, out_shape, in_specs, *args, out_specs=None, scratch=()):
+def call(body, name, out_shape, in_specs, *args, out_specs=None, scratch=(), room=16 * MIB):
     if out_specs is None:
         out_specs = [VMEM] * len(out_shape) if isinstance(out_shape, list) else VMEM
     return pl.pallas_call(
@@ -33,15 +34,24 @@
         in_specs=in_specs,
         out_specs=out_specs,
         scratch_shapes=scratch,
-        compiler_params=PARAMS,
+        compiler_params=pltpu.CompilerParams(vmem_limit_bytes=room),
         name=name,
     )(*args)
 
 
-def pack_inputs(raw, out):
-    heads = raw.shape[3]
-    blocks = raw[...].astype(f32)
-    rows = blocks[:, :ROWS].reshape(2 * BATCH, heads).astype(bf16)
+def pack_inputs(queries_hbm, fresh_hbm, gain_hbm, out, queries, fresh, gain, done):
+    copies = [
+        pltpu.make_async_copy(source, target, done.at[k])
+        for k, (source, target) in enumerate(
+            ((queries_hbm, queries), (fresh_hbm, fresh), (gain_hbm, gain))
+        )
+    ]
+    for copy in copies:
+        copy.start()
+    for copy in copies:
+        copy.wait()
+    heads = queries.shape[3]
+    rows = queries[...].astype(f32).reshape(2 * BATCH, heads).astype(bf16)
     entry = lax.broadcasted_iota(jnp.int32, (2 * BATCH, heads * BATCH), 0)
     target = lax.broadcasted_iota(jnp.int32, (2 * BATCH, heads * BATCH), 1)
     head = lax.broadcasted_iota(jnp.int32, (heads, heads * BATCH), 0)
@@ -59,8 +69,11 @@
             jnp.sum(jnp.where(lane // BATCH == head, spread, 0.0), axis=0, keepdims=True)
         )
     q = jnp.concatenate(lines, axis=0)
-    kv = [blocks[u, ROWS + w] for w in range(2) for u in range(STEPS)]
-    tail = kv + [blocks[0, ROWS + 2], blocks[0, ROWS + 3]] * 2
+    new = fresh[...].astype(f32)
+    kv = [new[u, w] for w in range(2) for u in range(STEPS)]
+    g = gain[...].astype(f32)
+    g = jnp.concatenate([g, g], axis=1)
+    tail = kv + [jnp.concatenate([g, g], axis=0)]
     half = q.shape[1] // 2
     lines = [
         jnp.concatenate([q[:, c * half : c * half + half]] + tail, axis=1).astype(bf16)
@@ -295,21 +308,19 @@
 
     count, page_len = kv_cache.shape[0], kv_cache.shape[2]
     tokens = 2 * count * page_len
-    raw = jnp.concatenate(
-        [
-            queries.transpose(0, 1, 3, 2),
-            fresh_kv[:, :, :, 0].transpose(0, 2, 3, 1),
-            lax.broadcast_in_dim(norm_gain[:ROWS], (STEPS, 1, 2, ROWS), (3,)),
-            lax.broadcast_in_dim(norm_gain[ROWS:], (STEPS, 1, 2, ROWS), (3,)),
-        ],
-        axis=1,
+    raw = (
+        queries.transpose(0, 1, 3, 2),
+        fresh_kv[:, :, :, 0].transpose(0, 2, 3, 1),
+        norm_gain.reshape(1, -1),
     )
     sent = call(
         pack_inputs,
         "pack_inputs",
         shape((kvp, 2, combos // 2 + 4 * BATCH), bf16),
-        [VMEM],
-        raw,
+        [HBM] * 3,
+        *raw,
+        scratch=[pltpu.VMEM(x.shape, bf16) for x in raw] + [pltpu.SemaphoreType.DMA((3,))],
+        room=ALL,
     )
     gathered = exchange(sent, "kvp")
     chips = kvp // 2

time: 106 us -> 105 us (level)
  no operation moved by 1% of the time
where the time goes in v6:
time: 105 us; the launch traced here: 104 us
  blocking collectives  79.9 us (76%)
  starting transfers between devices  10.7 us (10%)
  Pallas kernels  6.83 us (7%)
  waiting for transfers between devices  4.54 us (4%)
    all_to_all x5, blocking collectives, exchange(): lax.all_to_all(x, axis, split_axis=0, concat_axis=0, tiled=True, axis_ind...  77.5 us
    all_to_all x1, starting transfers between devices, exchange(): lax.all_to_all(x, axis, split_axis=0, concat_axis=0, tiled=True, axis_ind...  10.7 us
    pallas_call x8, Pallas kernels, call(): pl.pallas_call(body, out_shape=out_shape, in_specs=in_specs, out_specs=ou...  6.83 us
    all_to_all x1, waiting for transfers between devices, exchange(): lax.all_to_all(x, axis, split_axis=0, concat_axis=0, tiled=True, axis_ind...  4.54 us
    all_gather x1, blocking collectives, shards(): pages = lax.all_gather(kv_cache, 'kvp', axis_index_groups=same_chip)  2.38 us
  transfers between devices with their start and end apart: 1, of which 1 were waited for; matrix products, arithmetic and copies ran while one was open for 1% of the time, Pallas kernels for 1%

profile of v6, /device:TPU:8, one launch (start us, length us, event | category | flops | bytes accessed | tf_op | source)
XLA Modules:
  0.0 104.1 jit_solution(3426681374664056375)
XLA Ops:
  0.6 1.6 %pack_inputs.1 = bf16[64,2,384]{2,1,0:T(2,128)(2,1)} custom-call(bf16[2,16,2,16]{3,2,1,0:T(2,128)(2,1)} %bitcast.8, bf16[2,2,2,16]{3,2,1,0:T(2,128)(2,1)} %bitcast.9, bf16[1,32]{1,0:T(2,128)(2,1)} %bitcast.10), custom_call_target="tpu_custom_call" | custom-call | tf_op jit(solution)/shard_map/pack_inputs/pallas_call | solution.py:31
  2.3 0.0 copy-start.2
  2.3 10.7 %all-to-all-start = ((bf16[64,2,384]{2,1,0:T(2,128)(2,1)}), bf16[64,2,384]{2,1,0:T(2,128)(2,1)S(1)}, u32[]{:S(2)}, u32[]{:S(2)}) async-start(bf16[64,2,384]{2,1,0:T(2,128)(2,1)} %pack_inputs.1), calls=%async_computation | async-start | bytes 196608 | tf_op jit(solution)/shard_map/all_to_all | solution.py:287
  13.0 0.8 pad_add_fusion.numbers
  13.8 2.4 %all-gather = bf16[128,2,8,128]{3,2,1,0:T(8,128)(2,1)S(1)} all-gather(bf16[64,2,8,128]{3,2,1,0:T(8,128)(2,1)} %param.12), channel_id=2, replica_groups={{0,8},{16,24},{32,40},{48,56},{64,72},{80,88},{96,104},{112,120},{128,1..., dimensions={0}, use_global_device_ids=true | all-gather | bytes 786432 | tf_op jit(solution)/shard_map/all_gather | solution.py:330
  16.2 0.0 copy-start.3
  16.2 0.7 copy-done.3
  16.9 1.1 %prepare.1 = (bf16[1024,128]{1,0:T(8,128)(2,1)S(1)}, bf16[1024,128]{1,0:T(8,128)(2,1)S(1)}, f32[64,1024]{1,0:T(8,128)S(1)}, bf16[64,16,128]{2,1,0:T(8,128)(2,1)S(1)}, f32[8,128]{1,0:T(8,128)S(1)}) custom-call(s32[4112]{0:T(1024)S(1)} %pad_add_fusion.numbers, bf16[2,64,2,8,128]{4,3,2,1,0:T(8,128)(2,1)S(1)} %bitcast.7, bf16[32,32]{1,0:T(8,128)(2,1)S(1)} %copy-done.3), custom_call_target="tpu_custom_call" | custom-call | tf_op jit(solution)/shard_map/prepare/pallas_call | solution.py:31
  18.0 4.5 %all-to-all-done.gathered = bf16[64,2,384]{2,1,0:T(2,128)(2,1)S(1)} async-done(((bf16[64,2,384]{2,1,0:T(2,128)(2,1)}), bf16[64,2,384]{2,1,0:T(2,128)(2,1)S(1)}, u32[]{:S(2)}, u32[]{:S(2)}) %all-to-all-start) | async-done | bytes 98336 | tf_op jit(solution)/shard_map/all_to_all | solution.py:287
  22.5 0.0 copy-start
  22.5 0.0 copy-start.1
  22.5 1.1 %attention.1 = (bf16[32,3,4,128]{3,2,1,0:T(4,128)(2,1)S(1)}, f32[64,128]{1,0:T(8,128)S(1)}) custom-call(bf16[64,2,384]{2,1,0:T(2,128)(2,1)S(1)} %all-to-all-done.gathered, bf16[1024,128]{1,0:T(8,128)(2,1)S(1)} %get-tuple-element.15.key_ref, bf16[1024,128]{1,0:T(8,128)(2,1)S(1)} %get-tuple-element.16.value_ref, f32[64,1024]{1,0:T(8,128)S(1)} %get-tuple-element.17.member_ref), custom_call_target="tpu_custom_call" | custom-call | tf_op jit(solution)/shard_map/attention/pallas_call | solution.py:31
  23.6 14.7 %all_to_all.30.parts = bf16[32,3,4,128]{3,2,1,0:T(4,128)(2,1)S(1)} all-to-all(bf16[32,3,4,128]{3,2,1,0:T(4,128)(2,1)S(1)} %get-tuple-element.18), channel_id=1, replica_groups={{0,16,32,48,64,80,96,112,128,144,160,176,192,208,224,240,256,272,288,30..., dimensions={0} | all-to-all | bytes 196608 | tf_op jit(solution)/shard_map/all_to_all | solution.py:287
  38.3 0.3 merge.1
  38.5 18.6 %all_to_all.31.attended.pages = bf16[64,24,128]{2,1,0:T(8,128)(2,1)S(1)} all-to-all(bf16[64,24,128]{2,1,0:T(8,128)(2,1)S(1)} %merge.1), channel_id=1, replica_groups=mesh['kvp'=64,'tp'=8] {'kvp'}, dimensions={0} | all-to-all | bytes 786432 | tf_op jit(solution)/shard_map/all_to_all | solution.py:287
  57.1 0.0 copy-done.2
  57.1 0.4 project.1
  57.5 18.1 %all_to_all.32.parts = bf16[16,8,128]{2,1,0:T(8,128)(2,1)S(1)} all-to-all(bf16[16,8,128]{2,1,0:T(8,128)(2,1)S(1)} %project.1), channel_id=1, replica_groups={{0,1,2,3,4,5,6,7,8,9,10,11,12,13,14,15},{16,17,18,19,20,21,22,23,24,25,..., dimensions={0} | all-to-all | bytes 65536 | tf_op jit(solution)/shard_map/all_to_all | solution.py:287
  75.6 15.3 %all_to_all.33.columns = bf16[32,16,128]{2,1,0:T(8,128)(2,1)S(1)} all-to-all(bf16[32,16,128]{2,1,0:T(8,128)(2,1)S(1)} %get-tuple-element.21), channel_id=1, replica_groups={{0,16,32,48,64,80,96,112,128,144,160,176,192,208,224,240,256,272,288,30..., dimensions={0} | all-to-all | bytes 262144 | tf_op jit(solution)/shard_map/all_to_all | solution.py:287
  91.0 0.0 copy-done
  91.0 0.0 copy-done.1
  91.0 1.6 %feed_forward.1 = (bf16[8,32,128]{2,1,0:T(8,128)(2,1)S(1)}, bf16[32,32]{1,0:T(8,128)(2,1)}, bf16[64,16,128]{2,1,0:T(8,128)(2,1)}) custom-call(bf16[32,16,128]{2,1,0:T(8,128)(2,1)S(1)} %all_to_all.33.columns, f32[64,128]{1,0:T(8,128)S(1)} %get-tuple-element.22.gain, bf16[64,32,416]{2,1,0:T(8,128)(2,1)S(1)} %copy-done, bf16[64,32,416]{2,1,0:T(8,128)(2,1)S(1)} %copy-done.1, ...), custom_call_target="tpu_custom_call" | custom-call | tf_op jit(solution)/shard_map/feed_forward/pallas_call | solution.py:31
  92.6 10.8 %all_to_all.34.parts = bf16[8,32,128]{2,1,0:T(8,128)(2,1)S(1)} all-to-all(bf16[8,32,128]{2,1,0:T(8,128)(2,1)S(1)} %get-tuple-element.26), channel_id=1, replica_groups=mesh['kvp'=64,'tp'=8] {'tp'}, dimensions={0} | all-to-all | bytes 131072 | tf_op jit(solution)/shard_map/all_to_all | solution.py:287
  103.3 0.8 activate.1
  (1 shorter events, 0.0 us)
Async XLA Ops:
  2.3 54.9 %copy-start.2 = (bf16[2048,256]{1,0:T(8,128)(2,1)S(1)}, bf16[2048,256]{1,0:T(8,128)(2,1)}, u32[]{:S(2)}) copy-start(bf16[2048,256]{1,0:T(8,128)(2,1)} %weight.1) | copy-start | bytes 3145732
  2.3 20.3 %all-to-all-start = ((bf16[64,2,384]{2,1,0:T(2,128)(2,1)}), bf16[64,2,384]{2,1,0:T(2,128)(2,1)S(1)}, u32[]{:S(2)}, u32[]{:S(2)}) async-start(bf16[64,2,384]{2,1,0:T(2,128)(2,1)} %pack_inputs.1), calls=%async_computation | async-start | bytes 196608 | tf_op jit(solution)/shard_map/all_to_all | solution.py:287
  16.2 0.7 copy-start.3
  22.5 68.5 %copy-start = (bf16[64,32,416]{2,1,0:T(8,128)(2,1)S(1)}, bf16[64,32,416]{2,1,0:T(8,128)(2,1)}, u32[]{:S(2)}) copy-start(bf16[64,32,416]{2,1,0:T(8,128)(2,1)} %gate_weight.1) | copy-start | bytes 5111812
  22.5 68.5 %copy-start.1 = (bf16[64,32,416]{2,1,0:T(8,128)(2,1)S(1)}, bf16[64,32,416]{2,1,0:T(8,128)(2,1)}, u32[]{:S(2)}) copy-start(bf16[64,32,416]{2,1,0:T(8,128)(2,1)} %up_weight.1) | copy-start | bytes 5111812

commit v7 on v6

--- a/solution.py
+++ b/solution.py
@@ -13,6 +13,7 @@
 ROWS = 16
 BATCH = STEPS * ROWS
 LINES = 4 * ROWS
+UNROLL = 64
 
 negative = -1e30
 epsilon = 1e-05
@@ -104,11 +105,17 @@
     member[...] = jnp.where(row[:1] == line, 1.0, 0.0)
     packed[...] = pack(residual[...].astype(f32))
 
+    first = ROWS + me // 2 * 2 * count
+
     def one(c, carry):
-        ordered[numbers[ROWS + me * count + c]] = pages[me % 2, c].reshape(2 * page_len, HD)
+        for core in range(2):
+            place = numbers[first + core * count + c]
+            ordered[place, core * 2 * page_len : (core + 1) * 2 * page_len] = pages[
+                core, c
+            ].reshape(2 * page_len, HD)
         return carry
 
-    lax.fori_loop(0, count, one, 0, unroll=8)
+    lax.fori_loop(0, count, one, 0, unroll=UNROLL)
 
 
 def attention(gathered, key_ref, value_ref, member_ref, out, gain_out):
@@ -188,7 +195,7 @@
         values.append(numerator / jnp.sum(factor * total, axis=0))
     value = jnp.concatenate(values, axis=0).astype(bf16)
     value = jnp.broadcast_to(value[None], (out.shape[0],) + value.shape)
-    out[...] = jnp.concatenate([ordered[...], value], axis=1)
+    out[...] = jnp.concatenate([ordered[: out.shape[0]], value], axis=1)
 
 
 def pack(x):
@@ -196,9 +203,7 @@
 
 
 def project(attended, weight, residual, out):
-    x = attended[...][:, 16:].astype(f32).reshape(-1, 2, 8, HD)
-    x = jnp.concatenate([x[:, c].reshape(-1, BATCH, HD) for c in range(2)], axis=0)
-    x = x.astype(bf16)
+    x = attended[...].astype(f32).reshape(-1, BATCH, HD).astype(bf16)
     flat = jnp.concatenate([x[h] for h in range(x.shape[0])], axis=1)
     acc = jnp.dot(flat, weight[...], preferred_element_type=f32)
     tp = out.shape[0] // 2
@@ -327,6 +332,11 @@
     chip_line = [[chip * 2 * tp + k for k in range(2 * tp)] for chip in range(chips)]
     same_core = [[2 * chip + core for chip in range(chips)] for core in range(2)]
     same_chip = [[2 * chip, 2 * chip + 1] for chip in range(chips)]
+    numbers = jnp.concatenate([context_pages, page_owner])
+    mine = (numbers ^ lax.axis_index("kvp")) & 1 == 0
+    place = jnp.where(mine, numbers >> 1, chips)
+    index = lax.iota(jnp.int32, numbers.shape[0])
+    numbers = jnp.where(index < ROWS, numbers, place)
     pages = lax.all_gather(kv_cache, "kvp", axis_index_groups=same_chip)
     keys, values, member, ordered, packed = call(
         prepare,
@@ -335,11 +345,11 @@
             shape((tokens, HD), bf16),
             shape((tokens, HD), bf16),
             shape((LINES, tokens), f32),
-            shape((count, 2 * page_len, HD), bf16),
+            shape((chips + 1, 4 * page_len, HD), bf16),
             shape((8, HD), f32),
         ],
         [SMEM, VMEM, VMEM],
-        jnp.concatenate([context_pages, page_owner]),
+        numbers,
         pages,
         residual,
     )
@@ -357,12 +367,15 @@
     piece = call(
         merge,
         "merge",
-        shape((kvp, 2 * page_len + 8, HD), bf16),
+        shape((chips, 4 * page_len + 8, HD), bf16),
         [VMEM] * 2,
         parts,
         ordered,
     )
-    attended = exchange(piece, "kvp")
+    arrived = exchange(piece, "kvp", same_core)
+    attended = lax.all_gather(
+        arrived[:, 4 * page_len :], "kvp", axis_index_groups=same_chip
+    )
     partial = call(
         project,
         "project",
@@ -387,7 +400,7 @@
         [
             shape((tp, BATCH, HD), bf16),
             shape(residual.shape, bf16),
-            shape((count, 2 * page_len, HD), bf16),
+            shape((chips, 4 * page_len, HD), bf16),
         ],
         [VMEM] * 6,
         columns,
@@ -395,7 +408,7 @@
         gate_weight,
         up_weight,
         own,
-        attended,
+        arrived,
         out_specs=[VMEM, HBM, HBM],
         scratch=[pltpu.VMEM(residual.shape, bf16), pltpu.SemaphoreType.DMA((2,))],
     )

time: 105 us -> 103 us (0.981)
  blocking collectives: 79.9 us -> 78.5 us
    all_to_all x5, blocking collectives: 77.5 us -> 74.2 us  [exchange(): lax.all_to_all(x, axis, split_axis=0, concat_axis=0, tiled=True, axis_ind...]
    all_gather x0 -> x1, blocking collectives: none -> 1.89 us  [shards(): lax.all_gather(arrived[:, 4 * page_len:], 'kvp', axis_index_groups=same_c...]
where the time goes in v7:
time: 103 us
  blocking collectives  78.5 us (76%)
  starting transfers between devices  10.6 us (10%)
  Pallas kernels  6.77 us (7%)
  waiting for transfers between devices  4.5 us (4%)
    all_to_all x5, blocking collectives, exchange(): lax.all_to_all(x, axis, split_axis=0, concat_axis=0, tiled=True, axis_ind...  74.2 us
    all_to_all x1, starting transfers between devices, exchange(): lax.all_to_all(x, axis, split_axis=0, concat_axis=0, tiled=True, axis_ind...  10.6 us
    pallas_call x8, Pallas kernels, call(): pl.pallas_call(body, out_shape=out_shape, in_specs=in_specs, out_specs=ou...  6.77 us
    all_to_all x1, waiting for transfers between devices, exchange(): lax.all_to_all(x, axis, split_axis=0, concat_axis=0, tiled=True, axis_ind...  4.5 us
    all_gather x1, blocking collectives, shards(): pages = lax.all_gather(kv_cache, 'kvp', axis_index_groups=same_chip)  2.38 us
  transfers between devices with their start and end apart: 1, of which 1 were waited for; matrix products, arithmetic and copies ran while one was open for 1% of the time, Pallas kernels for 1%

profile of v7, /device:TPU:8, one launch (start us, length us, event | category | flops | bytes accessed | tf_op | source)
XLA Modules:
  0.0 102.6 jit_solution(11543595732693213199)
XLA Ops:
  0.6 1.6 %pack_inputs.1 = bf16[64,2,384]{2,1,0:T(2,128)(2,1)} custom-call(bf16[2,16,2,16]{3,2,1,0:T(2,128)(2,1)} %bitcast.10, bf16[2,2,2,16]{3,2,1,0:T(2,128)(2,1)} %bitcast.11, bf16[1,32]{1,0:T(2,128)(2,1)} %bitcast.12), custom_call_target="tpu_custom_call" | custom-call | tf_op jit(solution)/shard_map/pack_inputs/pallas_call | solution.py:32
  2.3 10.6 %all-to-all-start = ((bf16[64,2,384]{2,1,0:T(2,128)(2,1)}), bf16[64,2,384]{2,1,0:T(2,128)(2,1)S(1)}, u32[]{:S(2)}, u32[]{:S(2)}) async-start(bf16[64,2,384]{2,1,0:T(2,128)(2,1)} %pack_inputs.1), calls=%async_computation | async-start | bytes 196608 | tf_op jit(solution)/shard_map/all_to_all | solution.py:292
  12.8 0.0 copy-start.2
  12.9 0.9 select_select_fusion.numbers
  13.7 2.4 %all-gather = bf16[128,2,8,128]{3,2,1,0:T(8,128)(2,1)S(1)} all-gather(bf16[64,2,8,128]{3,2,1,0:T(8,128)(2,1)} %param.12), channel_id=2, replica_groups={{0,8},{16,24},{32,40},{48,56},{64,72},{80,88},{96,104},{112,120},{128,1..., dimensions={0}, use_global_device_ids=true | all-gather | bytes 786432 | tf_op jit(solution)/shard_map/all_gather | solution.py:340
  16.1 0.0 copy-start.3
  16.1 0.7 copy-done.3
  16.8 1.1 %prepare.1 = (bf16[1024,128]{1,0:T(8,128)(2,1)S(1)}, bf16[1024,128]{1,0:T(8,128)(2,1)S(1)}, f32[64,1024]{1,0:T(8,128)S(1)}, bf16[33,32,128]{2,1,0:T(8,128)(2,1)S(1)}, f32[8,128]{1,0:T(8,128)S(1)}) custom-call(s32[4112]{0:T(1024)S(1)} %select_select_fusion.numbers, bf16[2,64,2,8,128]{4,3,2,1,0:T(8,128)(2,1)S(1)} %bitcast.8, bf16[32,32]{1,0:T(8,128)(2,1)S(1)} %copy-done.3), custom_call_target="tpu_custom_call" | custom-call | tf_op jit(solution)/shard_map/prepare/pallas_call | solution.py:32
  17.9 4.5 %all-to-all-done.gathered = bf16[64,2,384]{2,1,0:T(2,128)(2,1)S(1)} async-done(((bf16[64,2,384]{2,1,0:T(2,128)(2,1)}), bf16[64,2,384]{2,1,0:T(2,128)(2,1)S(1)}, u32[]{:S(2)}, u32[]{:S(2)}) %all-to-all-start) | async-done | bytes 98336 | tf_op jit(solution)/shard_map/all_to_all | solution.py:292
  22.4 0.0 copy-start
  22.4 0.0 copy-start.1
  22.4 1.1 %attention.1 = (bf16[32,3,4,128]{3,2,1,0:T(4,128)(2,1)S(1)}, f32[64,128]{1,0:T(8,128)S(1)}) custom-call(bf16[64,2,384]{2,1,0:T(2,128)(2,1)S(1)} %all-to-all-done.gathered, bf16[1024,128]{1,0:T(8,128)(2,1)S(1)} %get-tuple-element.15.key_ref, bf16[1024,128]{1,0:T(8,128)(2,1)S(1)} %get-tuple-element.16.value_ref, f32[64,1024]{1,0:T(8,128)S(1)} %get-tuple-element.17.member_ref), custom_call_target="tpu_custom_call" | custom-call | tf_op jit(solution)/shard_map/attention/pallas_call | solution.py:32
  23.4 14.7 %all_to_all.30.parts = bf16[32,3,4,128]{3,2,1,0:T(4,128)(2,1)S(1)} all-to-all(bf16[32,3,4,128]{3,2,1,0:T(4,128)(2,1)S(1)} %get-tuple-element.18), channel_id=1, replica_groups={{0,16,32,48,64,80,96,112,128,144,160,176,192,208,224,240,256,272,288,30..., dimensions={0} | all-to-all | bytes 196608 | tf_op jit(solution)/shard_map/all_to_all | solution.py:292
  38.2 0.3 merge.1
  38.4 16.7 %all_to_all.31.pages = bf16[32,40,128]{2,1,0:T(8,128)(2,1)S(1)} all-to-all(bf16[32,40,128]{2,1,0:T(8,128)(2,1)S(1)} %merge.1), channel_id=1, replica_groups={{0,16,32,48,64,80,96,112,128,144,160,176,192,208,224,240,256,272,288,30..., dimensions={0} | all-to-all | bytes 655360 | tf_op jit(solution)/shard_map/all_to_all | solution.py:292
  55.1 1.9 %all-gather.1 = bf16[64,8,128]{2,1,0:T(8,128)(2,1)S(1)} all-gather(bf16[32,8,128]{2,1,0:T(8,128)(2,1)S(1)} %slice.4), channel_id=3, replica_groups={{0,8},{16,24},{32,40},{48,56},{64,72},{80,88},{96,104},{112,120},{128,1..., dimensions={0}, use_global_device_ids=true | all-gather | bytes 196608 | tf_op jit(solution)/shard_map/all_gather | solution.py:376
  57.0 0.0 copy-done.2
  57.0 0.4 project.1
  57.4 17.9 %all_to_all.32.parts = bf16[16,8,128]{2,1,0:T(8,128)(2,1)S(1)} all-to-all(bf16[16,8,128]{2,1,0:T(8,128)(2,1)S(1)} %project.1), channel_id=1, replica_groups={{0,1,2,3,4,5,6,7,8,9,10,11,12,13,14,15},{16,17,18,19,20,21,22,23,24,25,..., dimensions={0} | all-to-all | bytes 65536 | tf_op jit(solution)/shard_map/all_to_all | solution.py:292
  75.3 14.2 %all_to_all.33.columns = bf16[32,16,128]{2,1,0:T(8,128)(2,1)S(1)} all-to-all(bf16[32,16,128]{2,1,0:T(8,128)(2,1)S(1)} %get-tuple-element.21), channel_id=1, replica_groups={{0,16,32,48,64,80,96,112,128,144,160,176,192,208,224,240,256,272,288,30..., dimensions={0} | all-to-all | bytes 262144 | tf_op jit(solution)/shard_map/all_to_all | solution.py:292
  89.5 0.0 copy-done
  89.5 0.0 copy-done.1
  89.5 1.6 %feed_forward.1 = (bf16[8,32,128]{2,1,0:T(8,128)(2,1)S(1)}, bf16[32,32]{1,0:T(8,128)(2,1)}, bf16[32,32,128]{2,1,0:T(8,128)(2,1)}) custom-call(bf16[32,16,128]{2,1,0:T(8,128)(2,1)S(1)} %all_to_all.33.columns, f32[64,128]{1,0:T(8,128)S(1)} %get-tuple-element.22.gain, bf16[64,32,416]{2,1,0:T(8,128)(2,1)S(1)} %copy-done, bf16[64,32,416]{2,1,0:T(8,128)(2,1)S(1)} %copy-done.1, ...), custom_call_target="tpu_custom_call" | custom-call | tf_op jit(solution)/shard_map/feed_forward/pallas_call | solution.py:32
  91.1 10.8 %all_to_all.34.parts = bf16[8,32,128]{2,1,0:T(8,128)(2,1)S(1)} all-to-all(bf16[8,32,128]{2,1,0:T(8,128)(2,1)S(1)} %get-tuple-element.26), channel_id=1, replica_groups=mesh['kvp'=64,'tp'=8] {'tp'}, dimensions={0} | all-to-all | bytes 131072 | tf_op jit(solution)/shard_map/all_to_all | solution.py:292
  101.8 0.8 activate.1
  (2 shorter events, 0.0 us)
Async XLA Ops:
  2.3 20.1 %all-to-all-start = ((bf16[64,2,384]{2,1,0:T(2,128)(2,1)}), bf16[64,2,384]{2,1,0:T(2,128)(2,1)S(1)}, u32[]{:S(2)}, u32[]{:S(2)}) async-start(bf16[64,2,384]{2,1,0:T(2,128)(2,1)} %pack_inputs.1), calls=%async_computation | async-start | bytes 196608 | tf_op jit(solution)/shard_map/all_to_all | solution.py:292
  12.8 44.2 %copy-start.2 = (bf16[2048,256]{1,0:T(8,128)(2,1)S(1)}, bf16[2048,256]{1,0:T(8,128)(2,1)}, u32[]{:S(2)}) copy-start(bf16[2048,256]{1,0:T(8,128)(2,1)} %weight.1) | copy-start | bytes 3145732
  16.1 0.7 copy-start.3
  22.4 67.1 %copy-start = (bf16[64,32,416]{2,1,0:T(8,128)(2,1)S(1)}, bf16[64,32,416]{2,1,0:T(8,128)(2,1)}, u32[]{:S(2)}) copy-start(bf16[64,32,416]{2,1,0:T(8,128)(2,1)} %gate_weight.1) | copy-start | bytes 5111812
  22.4 67.1 %copy-start.1 = (bf16[64,32,416]{2,1,0:T(8,128)(2,1)S(1)}, bf16[64,32,416]{2,1,0:T(8,128)(2,1)}, u32[]{:S(2)}) copy-start(bf16[64,32,416]{2,1,0:T(8,128)(2,1)} %up_weight.1) | copy-start | bytes 5111812

commit v8 on v7

--- a/solution.py
+++ b/solution.py
@@ -40,12 +40,12 @@
     )(*args)
 
 
-def pack_inputs(queries_hbm, fresh_hbm, gain_hbm, out, queries, fresh, gain, done):
+def pack_inputs(*refs):
+    sources, (out, table), targets, done = refs[:6], refs[6:8], refs[8:14], refs[14]
+    queries, fresh, gain, residual, owner, context = targets
     copies = [
         pltpu.make_async_copy(source, target, done.at[k])
-        for k, (source, target) in enumerate(
-            ((queries_hbm, queries), (fresh_hbm, fresh), (gain_hbm, gain))
-        )
+        for k, (source, target) in enumerate(zip(sources, targets))
     ]
     for copy in copies:
         copy.start()
@@ -82,10 +82,26 @@
     ]
     sent = jnp.stack(lines, axis=0)[None]
     out[...] = jnp.broadcast_to(sent, (out.shape[0] // 2,) + sent.shape[1:]).reshape(out.shape)
+    me = lax.axis_index("kvp")
+    line = lax.broadcasted_iota(jnp.int32, owner.shape, 0)
+    to = jnp.sum(jnp.where(line == me // 2, owner[...], 0), axis=0, keepdims=True)
+    place = jnp.where((to ^ me) & 1 == 0, to >> 1, owner.shape[0])
+    spans = jnp.concatenate(
+        [context[...], jnp.zeros((1, HD - context.shape[1]), jnp.int32)], axis=1
+    )
+    table[...] = jnp.concatenate(
+        [
+            pack(residual[...].astype(f32)),
+            place.astype(f32),
+            spans.astype(f32),
+            jnp.zeros((6, HD), f32),
+        ],
+        axis=0,
+    )
 
 
 def prepare(
-    numbers, pages, residual, keys, values, member, ordered, packed
+    numbers, table, pages, keys, values, member, ordered, packed
 ):
     me = lax.axis_index("kvp")
     count, page_len = pages.shape[1], pages.shape[3]
@@ -99,17 +115,16 @@
     row = jnp.zeros(page.shape, jnp.int32)
     end = jnp.int32(0)
     for r in range(ROWS - 1):
-        end = end + numbers[r]
+        end = end + numbers[9, r].astype(jnp.int32)
         row = row + (page >= end).astype(jnp.int32)
     line = lax.broadcasted_iota(jnp.int32, member.shape, 0) % ROWS
     member[...] = jnp.where(row[:1] == line, 1.0, 0.0)
-    packed[...] = pack(residual[...].astype(f32))
-
-    first = ROWS + me // 2 * 2 * count
+    packed[...] = table[:8]
+
 
     def one(c, carry):
         for core in range(2):
-            place = numbers[first + core * count + c]
+            place = numbers[8, core * count + c].astype(jnp.int32)
             ordered[place, core * 2 * page_len : (core + 1) * 2 * page_len] = pages[
                 core, c
             ].reshape(2 * page_len, HD)
@@ -317,14 +332,17 @@
         queries.transpose(0, 1, 3, 2),
         fresh_kv[:, :, :, 0].transpose(0, 2, 3, 1),
         norm_gain.reshape(1, -1),
-    )
-    sent = call(
+        residual,
+        page_owner.reshape(-1, HD),
+        context_pages.reshape(1, -1),
+    )
+    sent, table = call(
         pack_inputs,
         "pack_inputs",
-        shape((kvp, 2, combos // 2 + 4 * BATCH), bf16),
-        [HBM] * 3,
+        [shape((kvp, 2, combos // 2 + 4 * BATCH), bf16), shape((16, HD), f32)],
+        [HBM] * 6,
         *raw,
-        scratch=[pltpu.VMEM(x.shape, bf16) for x in raw] + [pltpu.SemaphoreType.DMA((3,))],
+        scratch=[pltpu.VMEM(x.shape, x.dtype) for x in raw] + [pltpu.SemaphoreType.DMA((6,))],
         room=ALL,
     )
     gathered = exchange(sent, "kvp")
@@ -332,11 +350,6 @@
     chip_line = [[chip * 2 * tp + k for k in range(2 * tp)] for chip in range(chips)]
     same_core = [[2 * chip + core for chip in range(chips)] for core in range(2)]
     same_chip = [[2 * chip, 2 * chip + 1] for chip in range(chips)]
-    numbers = jnp.concatenate([context_pages, page_owner])
-    mine = (numbers ^ lax.axis_index("kvp")) & 1 == 0
-    place = jnp.where(mine, numbers >> 1, chips)
-    index = lax.iota(jnp.int32, numbers.shape[0])
-    numbers = jnp.where(index < ROWS, numbers, place)
     pages = lax.all_gather(kv_cache, "kvp", axis_index_groups=same_chip)
     keys, values, member, ordered, packed = call(
         prepare,
@@ -349,9 +362,9 @@
             shape((8, HD), f32),
         ],
         [SMEM, VMEM, VMEM],
-        numbers,
+        table,
+        table,
         pages,
-        residual,
     )
     parts, gain_rows = call(
         attention,

time: 103 us -> 102 us (level)
  transfers between devices with their start and end apart: 1 -> 1, of which waited for: 1 -> 1; matrix products, arithmetic and copies ran while one was open for 1% -> 0% of each run, Pallas kernels for 1% -> 1%
where the time goes in v8:
time: 102 us
  blocking collectives  77.9 us (76%)
  starting transfers between devices  10.6 us (10%)
  Pallas kernels  6.83 us (7%)
  waiting for transfers between devices  5.28 us (5%)
    all_to_all x5, blocking collectives, exchange(): lax.all_to_all(x, axis, split_axis=0, concat_axis=0, tiled=True, axis_ind...  73.4 us
    all_to_all x1, starting transfers between devices, exchange(): lax.all_to_all(x, axis, split_axis=0, concat_axis=0, tiled=True, axis_ind...  10.6 us
    pallas_call x8, Pallas kernels, call(): pl.pallas_call(body, out_shape=out_shape, in_specs=in_specs, out_specs=ou...  6.83 us
    all_to_all x1, waiting for transfers between devices, exchange(): lax.all_to_all(x, axis, split_axis=0, concat_axis=0, tiled=True, axis_ind...  5.28 us
    all_gather x1, blocking collectives, shards(): pages = lax.all_gather(kv_cache, 'kvp', axis_index_groups=same_chip)  2.52 us
  transfers between devices with their start and end apart: 1, of which 1 were waited for; matrix products, arithmetic and copies ran while one was open for 0% of the time, Pallas kernels for 1%

profile of v8, /device:TPU:8, one launch (start us, length us, event | category | flops | bytes accessed | tf_op | source)
XLA Modules:
  0.0 102.0 jit_solution(16315777420780983831)
XLA Ops:
  0.6 1.7 %pack_inputs.1 = (bf16[64,2,384]{2,1,0:T(2,128)(2,1)}, f32[16,128]{1,0:T(8,128)}) custom-call(bf16[2,16,2,16]{3,2,1,0:T(2,128)(2,1)} %bitcast.12, bf16[2,2,2,16]{3,2,1,0:T(2,128)(2,1)} %bitcast.14, bf16[1,32]{1,0:T(2,128)(2,1)} %bitcast.15, bf16[32,32]{1,0:T(8,128)(2,1)} %refs_3_.1, s32[32,128]{1,0:T(8,128)} %bitcast.13, s32[1,16]{1,0:T(1,128)} %bitcast.16), custom_call_target="tpu_custom_call" | custom-call | tf_op jit(solution)/shard_map/pack_inputs/pallas_call | solution.py:32
  2.4 10.6 %all-to-all-start = ((bf16[64,2,384]{2,1,0:T(2,128)(2,1)}), bf16[64,2,384]{2,1,0:T(2,128)(2,1)S(1)}, u32[]{:S(2)}, u32[]{:S(2)}) async-start(bf16[64,2,384]{2,1,0:T(2,128)(2,1)} %get-tuple-element.17), calls=%async_computation | async-start | bytes 196608 | tf_op jit(solution)/shard_map/all_to_all | solution.py:307
  12.9 0.0 copy-start.2
  13.0 2.5 %all-gather = bf16[128,2,8,128]{3,2,1,0:T(8,128)(2,1)S(1)} all-gather(bf16[64,2,8,128]{3,2,1,0:T(8,128)(2,1)} %param.12), channel_id=2, replica_groups={{0,8},{16,24},{32,40},{48,56},{64,72},{80,88},{96,104},{112,120},{128,1..., dimensions={0}, use_global_device_ids=true | all-gather | bytes 786432 | tf_op jit(solution)/shard_map/all_gather | solution.py:353
  15.5 0.0 copy-start.3
  15.5 0.7 copy-done.3
  16.2 1.0 prepare.1
  17.2 5.3 %all-to-all-done.gathered = bf16[64,2,384]{2,1,0:T(2,128)(2,1)S(1)} async-done(((bf16[64,2,384]{2,1,0:T(2,128)(2,1)}), bf16[64,2,384]{2,1,0:T(2,128)(2,1)S(1)}, u32[]{:S(2)}, u32[]{:S(2)}) %all-to-all-start) | async-done | bytes 98336 | tf_op jit(solution)/shard_map/all_to_all | solution.py:307
  22.5 0.0 copy-start
  22.5 0.0 copy-start.1
  22.5 1.1 %attention.1 = (bf16[32,3,4,128]{3,2,1,0:T(4,128)(2,1)S(1)}, f32[64,128]{1,0:T(8,128)S(1)}) custom-call(bf16[64,2,384]{2,1,0:T(2,128)(2,1)S(1)} %all-to-all-done.gathered, bf16[1024,128]{1,0:T(8,128)(2,1)S(1)} %get-tuple-element.19.key_ref, bf16[1024,128]{1,0:T(8,128)(2,1)S(1)} %get-tuple-element.20.value_ref, f32[64,1024]{1,0:T(8,128)S(1)} %get-tuple-element.21.member_ref), custom_call_target="tpu_custom_call" | custom-call | tf_op jit(solution)/shard_map/attention/pallas_call | solution.py:32
  23.5 13.9 %all_to_all.30.parts = bf16[32,3,4,128]{3,2,1,0:T(4,128)(2,1)S(1)} all-to-all(bf16[32,3,4,128]{3,2,1,0:T(4,128)(2,1)S(1)} %get-tuple-element.22), channel_id=1, replica_groups={{0,16,32,48,64,80,96,112,128,144,160,176,192,208,224,240,256,272,288,30..., dimensions={0} | all-to-all | bytes 196608 | tf_op jit(solution)/shard_map/all_to_all | solution.py:307
  37.5 0.3 merge.1
  37.8 16.7 %all_to_all.31.pages = bf16[32,40,128]{2,1,0:T(8,128)(2,1)S(1)} all-to-all(bf16[32,40,128]{2,1,0:T(8,128)(2,1)S(1)} %merge.1), channel_id=1, replica_groups={{0,16,32,48,64,80,96,112,128,144,160,176,192,208,224,240,256,272,288,30..., dimensions={0} | all-to-all | bytes 655360 | tf_op jit(solution)/shard_map/all_to_all | solution.py:307
  54.4 1.9 %all-gather.1 = bf16[64,8,128]{2,1,0:T(8,128)(2,1)S(1)} all-gather(bf16[32,8,128]{2,1,0:T(8,128)(2,1)S(1)} %slice.4), channel_id=3, replica_groups={{0,8},{16,24},{32,40},{48,56},{64,72},{80,88},{96,104},{112,120},{128,1..., dimensions={0}, use_global_device_ids=true | all-gather | bytes 196608 | tf_op jit(solution)/shard_map/all_gather | solution.py:389
  56.3 0.0 copy-done.2
  56.3 0.4 project.1
  56.7 17.9 %all_to_all.32.parts = bf16[16,8,128]{2,1,0:T(8,128)(2,1)S(1)} all-to-all(bf16[16,8,128]{2,1,0:T(8,128)(2,1)S(1)} %project.1), channel_id=1, replica_groups={{0,1,2,3,4,5,6,7,8,9,10,11,12,13,14,15},{16,17,18,19,20,21,22,23,24,25,..., dimensions={0} | all-to-all | bytes 65536 | tf_op jit(solution)/shard_map/all_to_all | solution.py:307
  74.6 14.2 %all_to_all.33.columns = bf16[32,16,128]{2,1,0:T(8,128)(2,1)S(1)} all-to-all(bf16[32,16,128]{2,1,0:T(8,128)(2,1)S(1)} %get-tuple-element.25), channel_id=1, replica_groups={{0,16,32,48,64,80,96,112,128,144,160,176,192,208,224,240,256,272,288,30..., dimensions={0} | all-to-all | bytes 262144 | tf_op jit(solution)/shard_map/all_to_all | solution.py:307
  88.8 0.0 copy-done
  88.8 0.0 copy-done.1
  88.8 1.6 %feed_forward.1 = (bf16[8,32,128]{2,1,0:T(8,128)(2,1)S(1)}, bf16[32,32]{1,0:T(8,128)(2,1)}, bf16[32,32,128]{2,1,0:T(8,128)(2,1)}) custom-call(bf16[32,16,128]{2,1,0:T(8,128)(2,1)S(1)} %all_to_all.33.columns, f32[64,128]{1,0:T(8,128)S(1)} %get-tuple-element.26.gain, bf16[64,32,416]{2,1,0:T(8,128)(2,1)S(1)} %copy-done, bf16[64,32,416]{2,1,0:T(8,128)(2,1)S(1)} %copy-done.1, ...), custom_call_target="tpu_custom_call" | custom-call | tf_op jit(solution)/shard_map/feed_forward/pallas_call | solution.py:32
  90.4 10.8 %all_to_all.34.parts = bf16[8,32,128]{2,1,0:T(8,128)(2,1)S(1)} all-to-all(bf16[8,32,128]{2,1,0:T(8,128)(2,1)S(1)} %get-tuple-element.30), channel_id=1, replica_groups=mesh['kvp'=64,'tp'=8] {'tp'}, dimensions={0} | all-to-all | bytes 131072 | tf_op jit(solution)/shard_map/all_to_all | solution.py:307
  101.1 0.8 activate.1
  (2 shorter events, 0.0 us)
Async XLA Ops:
  2.4 20.1 %all-to-all-start = ((bf16[64,2,384]{2,1,0:T(2,128)(2,1)}), bf16[64,2,384]{2,1,0:T(2,128)(2,1)S(1)}, u32[]{:S(2)}, u32[]{:S(2)}) async-start(bf16[64,2,384]{2,1,0:T(2,128)(2,1)} %get-tuple-element.17), calls=%async_computation | async-start | bytes 196608 | tf_op jit(solution)/shard_map/all_to_all | solution.py:307
  12.9 43.4 %copy-start.2 = (bf16[2048,256]{1,0:T(8,128)(2,1)S(1)}, bf16[2048,256]{1,0:T(8,128)(2,1)}, u32[]{:S(2)}) copy-start(bf16[2048,256]{1,0:T(8,128)(2,1)} %weight.1) | copy-start | bytes 3145732
  15.5 0.7 copy-start.3
  22.5 66.3 %copy-start = (bf16[64,32,416]{2,1,0:T(8,128)(2,1)S(1)}, bf16[64,32,416]{2,1,0:T(8,128)(2,1)}, u32[]{:S(2)}) copy-start(bf16[64,32,416]{2,1,0:T(8,128)(2,1)} %gate_weight.1) | copy-start | bytes 5111812
  22.5 66.3 %copy-start.1 = (bf16[64,32,416]{2,1,0:T(8,128)(2,1)S(1)}, bf16[64,32,416]{2,1,0:T(8,128)(2,1)}, u32[]{:S(2)}) copy-start(bf16[64,32,416]{2,1,0:T(8,128)(2,1)} %up_weight.1) | copy-start | bytes 5111812

commit v9 on v8

--- a/solution.py
+++ b/solution.py
@@ -210,7 +210,7 @@
         values.append(numerator / jnp.sum(factor * total, axis=0))
     value = jnp.concatenate(values, axis=0).astype(bf16)
     value = jnp.broadcast_to(value[None], (out.shape[0],) + value.shape)
-    out[...] = jnp.concatenate([ordered[: out.shape[0]], value], axis=1)
+    out[...] = jnp.concatenate([ordered[: out.shape[0], :16], value], axis=1)
 
 
 def pack(x):
@@ -230,12 +230,13 @@
     out[...] = jnp.stack(blocks * 2, axis=0).astype(bf16)
 
 
-def add_up(parts, own, sent):
+def add_up(parts, ordered, own, sent):
     total = jnp.sum(parts[...].astype(f32).reshape(2, -1, 8, HD), axis=1)
     value = total.reshape(16, HD).astype(bf16)
     wide = value.astype(f32)
     own[...] = jnp.where(lax.axis_index("kvp") % 2 == 0, wide[:8], wide[8:])
-    sent[...] = jnp.broadcast_to(value[None], sent.shape)
+    value = jnp.broadcast_to(value[None], (sent.shape[0],) + value.shape)
+    sent[...] = jnp.concatenate([value, ordered[: sent.shape[0], 16:]], axis=1)
 
 
 def feed_forward(
@@ -246,12 +247,13 @@
         [wide[:, 32 * q : 32 * q + 32] for q in range(4)], axis=0
     ).astype(bf16)
     copies = [
-        pltpu.make_async_copy(pages.at[:, : regrouped.shape[1]], regrouped, done.at[0]),
+        pltpu.make_async_copy(pages.at[:, :16], regrouped.at[:, :16], done.at[0]),
+        pltpu.make_async_copy(columns.at[:, 16:], regrouped.at[:, 16:], done.at[2]),
         pltpu.make_async_copy(staged, stream, done.at[1]),
     ]
     for copy in copies:
         copy.start()
-    x = columns[...].astype(f32).reshape(-1, 8, HD)
+    x = columns[:, :16].astype(f32).reshape(-1, 8, HD)
     square = jnp.sum(x * x, axis=0)
     square = jnp.concatenate(
         [jnp.sum(square[:, 32 * q : 32 * q + 32], axis=1, keepdims=True) for q in range(4)],
@@ -380,14 +382,14 @@
     piece = call(
         merge,
         "merge",
-        shape((chips, 4 * page_len + 8, HD), bf16),
+        shape((chips, 2 * page_len + 8, HD), bf16),
         [VMEM] * 2,
         parts,
         ordered,
     )
     arrived = exchange(piece, "kvp", same_core)
     attended = lax.all_gather(
-        arrived[:, 4 * page_len :], "kvp", axis_index_groups=same_chip
+        arrived[:, 2 * page_len :], "kvp", axis_index_groups=same_chip
     )
     partial = call(
         project,
@@ -402,9 +404,10 @@
     own, block = call(
         add_up,
         "add_up",
-        [shape((8, HD), f32), shape((chips, 16, HD), bf16)],
-        [VMEM],
+        [shape((8, HD), f32), shape((chips, 16 + 2 * page_len, HD), bf16)],
+        [VMEM] * 2,
         summands,
+        ordered,
     )
     columns = exchange(block, "kvp", same_core)
     lifted, stream, regrouped = call(
@@ -423,7 +426,7 @@
         own,
         arrived,
         out_specs=[VMEM, HBM, HBM],
-        scratch=[pltpu.VMEM(residual.shape, bf16), pltpu.SemaphoreType.DMA((2,))],
+        scratch=[pltpu.VMEM(residual.shape, bf16), pltpu.SemaphoreType.DMA((3,))],
     )
     lifted = exchange(lifted, "tp")
     hidden = call(

time: 102 us -> 102 us (level)
  no operation moved by 1% of the time
where the time goes in v9:
time: 102 us
  blocking collectives  77.5 us (76%)
  starting transfers between devices  10.6 us (10%)
  Pallas kernels  6.94 us (7%)
  waiting for transfers between devices  5.42 us (5%)
    all_to_all x5, blocking collectives, exchange(): lax.all_to_all(x, axis, split_axis=0, concat_axis=0, tiled=True, axis_ind...  73.2 us
    all_to_all x1, starting transfers between devices, exchange(): lax.all_to_all(x, axis, split_axis=0, concat_axis=0, tiled=True, axis_ind...  10.6 us
    pallas_call x8, Pallas kernels, call(): pl.pallas_call(body, out_shape=out_shape, in_specs=in_specs, out_specs=ou...  6.94 us
    all_to_all x1, waiting for transfers between devices, exchange(): lax.all_to_all(x, axis, split_axis=0, concat_axis=0, tiled=True, axis_ind...  5.42 us
    all_gather x1, blocking collectives, shards(): pages = lax.all_gather(kv_cache, 'kvp', axis_index_groups=same_chip)  2.39 us
  transfers between devices with their start and end apart: 1, of which 1 were waited for; matrix products, arithmetic and copies ran while one was open for 0% of the time, Pallas kernels for 1%

profile of v9, /device:TPU:8, one launch (start us, length us, event | category | flops | bytes accessed | tf_op | source)
XLA Modules:
  0.0 101.8 jit_solution(3171544575334530860)
XLA Ops:
  0.6 0.0 copy-start.2
  0.6 1.8 %pack_inputs.1 = (bf16[64,2,384]{2,1,0:T(2,128)(2,1)}, f32[16,128]{1,0:T(8,128)}) custom-call(bf16[2,16,2,16]{3,2,1,0:T(2,128)(2,1)} %bitcast.12, bf16[2,2,2,16]{3,2,1,0:T(2,128)(2,1)} %bitcast.14, bf16[1,32]{1,0:T(2,128)(2,1)} %bitcast.15, bf16[32,32]{1,0:T(8,128)(2,1)} %refs_3_.1, s32[32,128]{1,0:T(8,128)} %bitcast.13, s32[1,16]{1,0:T(1,128)} %bitcast.16), custom_call_target="tpu_custom_call" | custom-call | tf_op jit(solution)/shard_map/pack_inputs/pallas_call | solution.py:32
  2.4 10.6 %all-to-all-start = ((bf16[64,2,384]{2,1,0:T(2,128)(2,1)}), bf16[64,2,384]{2,1,0:T(2,128)(2,1)S(1)}, u32[]{:S(2)}, u32[]{:S(2)}) async-start(bf16[64,2,384]{2,1,0:T(2,128)(2,1)} %get-tuple-element.17), calls=%async_computation | async-start | bytes 196608 | tf_op jit(solution)/shard_map/all_to_all | solution.py:309
  13.0 2.4 %all-gather = bf16[128,2,8,128]{3,2,1,0:T(8,128)(2,1)S(1)} all-gather(bf16[64,2,8,128]{3,2,1,0:T(8,128)(2,1)} %param.12), channel_id=2, replica_groups={{0,8},{16,24},{32,40},{48,56},{64,72},{80,88},{96,104},{112,120},{128,1..., dimensions={0}, use_global_device_ids=true | all-gather | bytes 786432 | tf_op jit(solution)/shard_map/all_gather | solution.py:355
  15.4 0.0 copy-start.3
  15.4 0.7 copy-done.3
  16.1 1.0 %prepare.1 = (bf16[1024,128]{1,0:T(8,128)(2,1)S(1)}, bf16[1024,128]{1,0:T(8,128)(2,1)S(1)}, f32[64,1024]{1,0:T(8,128)S(1)}, bf16[33,32,128]{2,1,0:T(8,128)(2,1)S(1)}, f32[8,128]{1,0:T(8,128)S(1)}) custom-call(f32[16,128]{1,0:T(8,128)S(1)} %copy-done.3, f32[16,128]{1,0:T(8,128)S(1)} %copy-done.3, bf16[2,64,2,8,128]{4,3,2,1,0:T(8,128)(2,1)S(1)} %bitcast.10), custom_call_target="tpu_custom_call" | custom-call | tf_op jit(solution)/shard_map/prepare/pallas_call | solution.py:32
  17.2 5.4 %all-to-all-done.gathered = bf16[64,2,384]{2,1,0:T(2,128)(2,1)S(1)} async-done(((bf16[64,2,384]{2,1,0:T(2,128)(2,1)}), bf16[64,2,384]{2,1,0:T(2,128)(2,1)S(1)}, u32[]{:S(2)}, u32[]{:S(2)}) %all-to-all-start) | async-done | bytes 98336 | tf_op jit(solution)/shard_map/all_to_all | solution.py:309
  22.6 0.0 copy-start
  22.6 0.0 copy-start.1
  22.6 1.1 %attention.1 = (bf16[32,3,4,128]{3,2,1,0:T(4,128)(2,1)S(1)}, f32[64,128]{1,0:T(8,128)S(1)}) custom-call(bf16[64,2,384]{2,1,0:T(2,128)(2,1)S(1)} %all-to-all-done.gathered, bf16[1024,128]{1,0:T(8,128)(2,1)S(1)} %get-tuple-element.19.key_ref, bf16[1024,128]{1,0:T(8,128)(2,1)S(1)} %get-tuple-element.20.value_ref, f32[64,1024]{1,0:T(8,128)S(1)} %get-tuple-element.21.member_ref), custom_call_target="tpu_custom_call" | custom-call | tf_op jit(solution)/shard_map/attention/pallas_call | solution.py:32
  23.6 13.9 %all_to_all.30.parts = bf16[32,3,4,128]{3,2,1,0:T(4,128)(2,1)S(1)} all-to-all(bf16[32,3,4,128]{3,2,1,0:T(4,128)(2,1)S(1)} %get-tuple-element.22), channel_id=1, replica_groups={{0,16,32,48,64,80,96,112,128,144,160,176,192,208,224,240,256,272,288,30..., dimensions={0} | all-to-all | bytes 196608 | tf_op jit(solution)/shard_map/all_to_all | solution.py:309
  37.5 0.3 merge.1
  37.8 14.1 %all_to_all.31.pages = bf16[32,24,128]{2,1,0:T(8,128)(2,1)S(1)} all-to-all(bf16[32,24,128]{2,1,0:T(8,128)(2,1)S(1)} %merge.1), channel_id=1, replica_groups={{0,16,32,48,64,80,96,112,128,144,160,176,192,208,224,240,256,272,288,30..., dimensions={0} | all-to-all | bytes 393216 | tf_op jit(solution)/shard_map/all_to_all | solution.py:309
  51.9 1.9 %all-gather.1 = bf16[64,8,128]{2,1,0:T(8,128)(2,1)S(1)} all-gather(bf16[32,8,128]{2,1,0:T(8,128)(2,1)S(1)} %slice.4), channel_id=3, replica_groups={{0,8},{16,24},{32,40},{48,56},{64,72},{80,88},{96,104},{112,120},{128,1..., dimensions={0}, use_global_device_ids=true | all-gather | bytes 196608 | tf_op jit(solution)/shard_map/all_gather | solution.py:391
  53.8 0.0 copy-done.2
  53.8 0.4 project.1
  54.2 17.9 %all_to_all.32.parts = bf16[16,8,128]{2,1,0:T(8,128)(2,1)S(1)} all-to-all(bf16[16,8,128]{2,1,0:T(8,128)(2,1)S(1)} %project.1), channel_id=1, replica_groups={{0,1,2,3,4,5,6,7,8,9,10,11,12,13,14,15},{16,17,18,19,20,21,22,23,24,25,..., dimensions={0} | all-to-all | bytes 65536 | tf_op jit(solution)/shard_map/all_to_all | solution.py:309
  72.1 16.5 %all_to_all.33.columns = bf16[32,32,128]{2,1,0:T(8,128)(2,1)S(1)} all-to-all(bf16[32,32,128]{2,1,0:T(8,128)(2,1)S(1)} %get-tuple-element.25), channel_id=1, replica_groups={{0,16,32,48,64,80,96,112,128,144,160,176,192,208,224,240,256,272,288,30..., dimensions={0} | all-to-all | bytes 524288 | tf_op jit(solution)/shard_map/all_to_all | solution.py:309
  88.7 0.0 copy-done
  88.7 0.0 copy-done.1
  88.7 1.6 %feed_forward.1 = (bf16[8,32,128]{2,1,0:T(8,128)(2,1)S(1)}, bf16[32,32]{1,0:T(8,128)(2,1)}, bf16[32,32,128]{2,1,0:T(8,128)(2,1)}) custom-call(bf16[32,32,128]{2,1,0:T(8,128)(2,1)S(1)} %all_to_all.33.columns, f32[64,128]{1,0:T(8,128)S(1)} %get-tuple-element.26.gain, bf16[64,32,416]{2,1,0:T(8,128)(2,1)S(1)} %copy-done, bf16[64,32,416]{2,1,0:T(8,128)(2,1)S(1)} %copy-done.1, ...), custom_call_target="tpu_custom_call" | custom-call | tf_op jit(solution)/shard_map/feed_forward/pallas_call | solution.py:32
  90.3 10.8 %all_to_all.34.parts = bf16[8,32,128]{2,1,0:T(8,128)(2,1)S(1)} all-to-all(bf16[8,32,128]{2,1,0:T(8,128)(2,1)S(1)} %get-tuple-element.30), channel_id=1, replica_groups=mesh['kvp'=64,'tp'=8] {'tp'}, dimensions={0} | all-to-all | bytes 131072 | tf_op jit(solution)/shard_map/all_to_all | solution.py:309
  101.0 0.8 activate.1
  (2 shorter events, 0.0 us)
Async XLA Ops:
  0.6 53.2 %copy-start.2 = (bf16[2048,256]{1,0:T(8,128)(2,1)S(1)}, bf16[2048,256]{1,0:T(8,128)(2,1)}, u32[]{:S(2)}) copy-start(bf16[2048,256]{1,0:T(8,128)(2,1)} %weight.1) | copy-start | bytes 3145732
  2.4 20.1 %all-to-all-start = ((bf16[64,2,384]{2,1,0:T(2,128)(2,1)}), bf16[64,2,384]{2,1,0:T(2,128)(2,1)S(1)}, u32[]{:S(2)}, u32[]{:S(2)}) async-start(bf16[64,2,384]{2,1,0:T(2,128)(2,1)} %get-tuple-element.17), calls=%async_computation | async-start | bytes 196608 | tf_op jit(solution)/shard_map/all_to_all | solution.py:309
  15.4 0.7 copy-start.3
  22.6 66.1 %copy-start = (bf16[64,32,416]{2,1,0:T(8,128)(2,1)S(1)}, bf16[64,32,416]{2,1,0:T(8,128)(2,1)}, u32[]{:S(2)}) copy-start(bf16[64,32,416]{2,1,0:T(8,128)(2,1)} %gate_weight.1) | copy-start | bytes 5111812
  22.6 66.1 %copy-start.1 = (bf16[64,32,416]{2,1,0:T(8,128)(2,1)S(1)}, bf16[64,32,416]{2,1,0:T(8,128)(2,1)}, u32[]{:S(2)}) copy-start(bf16[64,32,416]{2,1,0:T(8,128)(2,1)} %up_weight.1) | copy-start | bytes 5111812
